TPU v7x, 32 devices: a whole 2x2x4 slice. The times are simulated.
32 devices in a mesh: clip: 8 (over z, y), head: 4 (over x, core).
Axes of the slice: x: 2, y: 2, z: 4, core: 2. Of those that a mesh axis runs over, the one named last changes fastest.
Arguments:
- patch_tokens: bfloat16 [8, 8, 196, 768], P('clip', 'head'), may hold values from -6 to 6
- class_token: bfloat16 [8, 768], P('clip'), may hold values from -6 to 6
- keep_mask: int32 [8, 8, 196], P('clip'), may hold values from 0 to 1, as said below
- patch_grad: bfloat16 [8, 8, 196, 768], P('clip', 'head'), may hold values from -6 to 6
- class_grad: bfloat16 [8, 768], P('clip'), may hold values from -6 to 6
- norm_gain: float32 [1, 3, 768], replicated, may hold values from 0.5 to 1.5
- norm_bias: float32 [1, 3, 768], replicated, may hold values from -1.75 to 1.75
- input_weight: bfloat16 [1, 2, 768, 3, 768], P(None, None, None, None, 'head'), may hold values from -0.21875 to 0.21875
- input_bias: float32 [1, 2, 2, 768], P(None, None, None, 'head'), may hold values from -1.75 to 1.75
- output_weight: bfloat16 [1, 2, 768, 768], P(None, None, 'head'), may hold values from -0.875 to 0.875
- time_mixer: bfloat16 [1, 768, 768], replicated, may hold values from -0.21875 to 0.21875
- output_bias: float32 [1, 4, 768], replicated, may hold values from -1.75 to 1.75
- hidden_weight: bfloat16 [1, 768, 3072], P(None, None, 'head'), may hold values from -0.21875 to 0.21875
- hidden_bias: float32 [1, 3072], P(None, 'head'), may hold values from -1.75 to 1.75
- return_weight: bfloat16 [1, 3072, 768], P(None, 'head'), may hold values from -0.109375 to 0.109375
Outputs:
- patch_out: float32 [8, 8, 196, 768], P('clip', 'head')
- class_out: float32 [8, 768], P('clip', 'head')
- patch_input_grad: float32 [8, 8, 196, 768], P('clip', 'head')
- class_input_grad: float32 [8, 768], P('clip', 'head')
- grad_norm_gain: float32 [1, 3, 768], P(None, None, ('clip', 'head'))
- grad_norm_bias: float32 [1, 3, 768], P(None, None, ('clip', 'head'))
- grad_input_weight: float32 [1, 2, 768, 3, 768], P(None, None, 'clip', None, 'head')
- grad_input_bias: float32 [1, 2, 2, 768], P(None, None, None, ('head', 'clip'))
- grad_output_weight: float32 [1, 2, 768, 768], P(None, None, 'head', 'clip')
- grad_time_mixer: float32 [1, 768, 768], P(None, ('clip', 'head'))
- grad_output_bias: float32 [1, 4, 768], P(None, None, ('clip', 'head'))
- grad_hidden_weight: float32 [1, 768, 3072], P(None, 'clip', 'head')
- grad_hidden_bias: float32 [1, 3072], P(None, ('head', 'clip'))
- grad_return_weight: float32 [1, 3072, 768], P(None, 'head', 'clip')
Inputs may be any that keep to these rules, and one draw needn't show every extreme that they name: `keep_mask`: 1 keeps the patch token, 0 drops it; the share kept differs from clip to clip and from frame to frame.
All inputs are finite; a program needn't handle non-finite values.
Results may differ from a plain program's by a relative error of at most 0.03.
Values may be sent and summed in bfloat16 or wider, within the bound.
A program may use at most 192 MiB of HBM per device.

v0:
```python
import jax
import jax.numpy as jnp
from jax import lax
from jax.sharding import PartitionSpec as P

HEAD_DIM = 64


EPSILON = 1e-06
MASKED = -1e30
FLOAT = jnp.float32
HALF = jnp.bfloat16


def layer_norm(values, gains, shifts):
    average = jnp.mean(values, axis=-1, keepdims=True)
    centred = values - average
    spread = jnp.mean(centred * centred, axis=-1, keepdims=True)
    return centred * lax.rsqrt(spread + EPSILON) * gains + shifts


def norm_back(values, gains, shifts, grads):
    return jax.vjp(layer_norm, values, gains, shifts)[1](grads)


def gelu_exact(values):
    return jax.nn.gelu(values, approximate=False)


def attend(queries, keys, values, allowed):
    scale = HEAD_DIM ** (-0.5)
    scores = jnp.einsum("...qd,...kd->...qk", queries, keys, preferred_element_type=FLOAT) * scale
    scores = jnp.where(allowed, scores, MASKED)
    row_max = jnp.max(scores, axis=-1, keepdims=True)
    exponent = jnp.exp(scores - row_max)
    totals = jnp.sum(exponent, axis=-1, keepdims=True)
    weights = (exponent / totals).astype(HALF)
    result = jnp.einsum("...qk,...kd->...qd", weights, values, preferred_element_type=FLOAT)
    return (result, row_max[..., 0] + jnp.log(totals[..., 0]))


def attend_back(queries, keys, values, allowed, log_total, out_grad):
    scale = HEAD_DIM ** (-0.5)
    scores = jnp.einsum("...qd,...kd->...qk", queries, keys, preferred_element_type=FLOAT) * scale
    weights = jnp.where(allowed, jnp.exp(scores - log_total[..., None]), 0.0)
    value_grad = jnp.einsum(
        "...qk,...qd->...kd", weights.astype(HALF), out_grad, preferred_element_type=FLOAT
    )
    weight_grad = jnp.einsum("...qd,...kd->...qk", out_grad, values, preferred_element_type=FLOAT)
    score_grad = (
        weights * (weight_grad - jnp.sum(weights * weight_grad, axis=-1, keepdims=True))
    ).astype(HALF)
    query_grad = (
        jnp.einsum("...qk,...kd->...qd", score_grad, keys, preferred_element_type=FLOAT) * scale
    )
    key_grad = (
        jnp.einsum("...qk,...qd->...kd", score_grad, queries, preferred_element_type=FLOAT) * scale
    )
    return (query_grad, key_grad, value_grad)


def arrange_rows(patch_full, class_part, part_count):
    clip_count, frame_count, patch_count, feature_count = patch_full.shape
    local_frames = frame_count // part_count
    grouped = patch_full.reshape(
        clip_count, part_count, local_frames * patch_count, feature_count
    ).transpose(1, 0, 2, 3)
    if class_part is not None:
        class_rows = jnp.broadcast_to(
            class_part[None, :, None, :], (part_count, clip_count, 1, feature_count)
        )
        grouped = jnp.concatenate([grouped, class_rows], axis=2)
    return grouped.reshape(-1, feature_count)


def split_rows(summed, local_shape):
    clip_count, local_frames, patch_count, feature_count = local_shape
    shaped = summed.reshape(clip_count, local_frames * patch_count + 1, feature_count)
    return (shaped[:, :-1].reshape(local_shape), shaped[:, -1])


def frame_sequences(patch_part, class_part, head_count):
    clip_count, frame_count, patch_count, feature_count = patch_part.shape
    class_rows = jnp.broadcast_to(
        class_part[:, None, None, :], (clip_count, frame_count, 1, feature_count)
    )
    joined = jnp.concatenate([class_rows, patch_part], axis=2)
    return joined.reshape(
        clip_count, frame_count, patch_count + 1, head_count, feature_count // head_count
    ).transpose(0, 1, 3, 2, 4)


def sequence_rows(sequences):
    clip_count, frame_count, head_count, token_count, head_width = sequences.shape
    return sequences.transpose(0, 1, 3, 2, 4).reshape(
        clip_count, frame_count, token_count, head_count * head_width
    )


def time_sequences(patch_part, head_count):
    clip_count, frame_count, patch_count, feature_count = patch_part.shape
    return patch_part.reshape(
        clip_count, frame_count, patch_count, head_count, feature_count // head_count
    ).transpose(0, 2, 3, 1, 4)


def time_rows(sequences):
    clip_count, patch_count, head_count, frame_count, head_width = sequences.shape
    return sequences.transpose(0, 3, 1, 2, 4).reshape(
        clip_count, frame_count, patch_count, head_count * head_width
    )


def project_inputs(rows, weight, biases):
    mixed = jnp.einsum("...d,dje->...je", rows, weight, preferred_element_type=FLOAT)
    bias_rows = jnp.stack([biases[0], jnp.zeros_like(biases[0]), biases[1]])
    return (mixed + bias_rows).astype(HALF)


def qkv_bias_grad(patch_part, class_part):
    totals = jnp.sum(patch_part.astype(FLOAT), axis=(0, 1, 2))
    if class_part is not None:
        totals = totals + jnp.sum(class_part.astype(FLOAT), axis=0)
    return jnp.stack([totals[0], totals[2]])


def gather_rows(normed):
    return lax.all_gather(normed, "head", axis=1, tiled=True)


def gather_grads(rows):
    return lax.all_gather(rows, "head", axis=1, tiled=True)


def forward_sum(arranged, weight):
    rows_here = lax.all_to_all(arranged, "head", split_axis=0, concat_axis=1, tiled=True)
    whole_weight = lax.all_gather(weight, "head", axis=0, tiled=True)
    return jnp.dot(rows_here, whole_weight, preferred_element_type=FLOAT)


def backward_sum(arranged, weight):
    rows_here = lax.all_to_all(arranged, "head", split_axis=0, concat_axis=1, tiled=True)
    whole_weight = lax.all_gather(weight, "head", axis=1, tiled=True)
    return lax.dot_general(
        rows_here, whole_weight, (((1,), (1,)), ((), ())), preferred_element_type=FLOAT
    )


def on_device(
    patch_tokens,
    class_token,
    keep_mask,
    patch_grad,
    class_grad,
    norm_gain,
    norm_bias,
    input_weight,
    input_bias,
    output_weight,
    time_mixer,
    output_bias,
    hidden_weight,
    hidden_bias,
    return_weight,
):
    part_count = lax.axis_size("head")
    head_index = lax.axis_index("head")
    clip_count, local_frames, patch_count, model_width = patch_tokens.shape
    frame_count = local_frames * part_count
    local_width = input_weight.shape[-1]
    local_heads = local_width // HEAD_DIM
    layer_count = input_weight.shape[0]
    first_part = (head_index == 0).astype(FLOAT)
    kept = keep_mask > 0
    kept_local = lax.dynamic_slice_in_dim(
        keep_mask, head_index * local_frames, local_frames, 1
    ).astype(FLOAT)[..., None]
    time_allowed = jnp.transpose(kept, (0, 2, 1))[:, :, None, None, :] | jnp.eye(
        frame_count, dtype=jnp.bool_
    )
    space_valid = jnp.concatenate([jnp.ones((clip_count, frame_count, 1), jnp.bool_), kept], axis=2)
    space_allowed = space_valid[:, :, None, None, :] | jnp.eye(patch_count + 1, dtype=jnp.bool_)
    patch_state = patch_tokens.astype(FLOAT)
    class_state = class_token.astype(FLOAT)
    layer_index = 0
    gains = norm_gain[layer_index]
    shifts = norm_bias[layer_index]
    biases = output_bias[layer_index]
    time_input = patch_state
    time_normed = gather_rows(layer_norm(patch_state, gains[0], shifts[0]).astype(HALF))
    time_qkv = project_inputs(time_normed, input_weight[layer_index, 0], input_bias[layer_index, 0])
    time_out, time_total = attend(
        time_sequences(time_qkv[..., 0, :], local_heads),
        time_sequences(time_qkv[..., 1, :], local_heads),
        time_sequences(time_qkv[..., 2, :], local_heads),
        time_allowed,
    )
    time_mixed = time_rows(time_out).astype(HALF)
    time_sum = forward_sum(
        arrange_rows(time_mixed, None, part_count), output_weight[layer_index, 0]
    )
    time_proj = (time_sum.reshape(patch_state.shape) + biases[0]).astype(HALF)
    patch_state = patch_state + (
        jnp.dot(time_proj, time_mixer[layer_index], preferred_element_type=FLOAT) + biases[1]
    )
    space_input = patch_state
    class_input = class_state
    space_normed = gather_rows(layer_norm(patch_state, gains[1], shifts[1]).astype(HALF))
    class_normed = layer_norm(class_state, gains[1], shifts[1]).astype(HALF)
    space_qkv = project_inputs(
        space_normed, input_weight[layer_index, 1], input_bias[layer_index, 1]
    )
    class_qkv = project_inputs(
        class_normed, input_weight[layer_index, 1], input_bias[layer_index, 1]
    )
    space_out, space_total = attend(
        frame_sequences(space_qkv[..., 0, :], class_qkv[:, 0], local_heads),
        frame_sequences(space_qkv[..., 1, :], class_qkv[:, 1], local_heads),
        frame_sequences(space_qkv[..., 2, :], class_qkv[:, 2], local_heads),
        space_allowed,
    )
    space_rows = sequence_rows(space_out)
    class_mixed = jnp.mean(space_rows[:, :, 0], axis=1).astype(HALF)
    patch_mixed = space_rows[:, :, 1:].astype(HALF)
    space_sum = forward_sum(
        arrange_rows(patch_mixed, class_mixed, part_count), output_weight[layer_index, 1]
    )
    patch_add, class_add = split_rows(space_sum, patch_state.shape)
    patch_state = patch_state + (patch_add + biases[2])
    class_state = class_state + (class_add + biases[2])
    mlp_input = patch_state
    mlp_class = class_state
    mlp_normed = gather_rows(layer_norm(patch_state, gains[2], shifts[2]).astype(HALF))
    class_mlp_normed = layer_norm(class_state, gains[2], shifts[2]).astype(HALF)
    hidden_rows = (
        jnp.dot(mlp_normed, hidden_weight[layer_index], preferred_element_type=FLOAT)
        + hidden_bias[layer_index]
    )
    hidden_class = (
        jnp.dot(class_mlp_normed, hidden_weight[layer_index], preferred_element_type=FLOAT)
        + hidden_bias[layer_index]
    )
    active_rows = gelu_exact(hidden_rows).astype(HALF)
    active_class = gelu_exact(hidden_class).astype(HALF)
    mlp_sum = forward_sum(
        arrange_rows(active_rows, active_class, part_count), return_weight[layer_index]
    )
    patch_add, class_add = split_rows(mlp_sum, patch_state.shape)
    patch_state = patch_state + (patch_add + biases[3])
    class_state = class_state + (class_add + biases[3])
    saved = [
        (
            time_input,
            time_normed,
            time_qkv,
            time_total,
            time_mixed,
            time_proj,
            space_input,
            class_input,
            space_normed,
            class_normed,
            space_qkv,
            class_qkv,
            space_total,
            patch_mixed,
            class_mixed,
            mlp_input,
            mlp_class,
            mlp_normed,
            class_mlp_normed,
            hidden_rows,
            hidden_class,
            active_rows,
            active_class,
        )
    ]
    patch_out = patch_state * kept_local
    width_part = model_width // part_count
    class_out = lax.dynamic_slice_in_dim(class_state, head_index * width_part, width_part, 1)
    patch_back = patch_grad.astype(FLOAT) * kept_local
    class_back = class_grad.astype(FLOAT)
    wide_parts = [None] * layer_count
    shared_parts = [None] * layer_count
    for layer_index in reversed(range(layer_count)):
        (
            time_input,
            time_normed,
            time_qkv,
            time_total,
            time_mixed,
            time_proj,
            space_input,
            class_input,
            space_normed,
            class_normed,
            space_qkv,
            class_qkv,
            space_total,
            patch_mixed,
            class_mixed,
            mlp_input,
            mlp_class,
            mlp_normed,
            class_mlp_normed,
            hidden_rows,
            hidden_class,
            active_rows,
            active_class,
        ) = saved[layer_index]
        gains = norm_gain[layer_index]
        shifts = norm_bias[layer_index]
        bias_three = jnp.sum(patch_back, axis=(0, 1, 2)) + first_part * jnp.sum(class_back, axis=0)
        mlp_grad = gather_grads(patch_back.astype(HALF))
        class_mlp_grad = class_back.astype(HALF)
        return_grad = jnp.einsum(
            "cfpm,cfpd->md", active_rows, mlp_grad, preferred_element_type=FLOAT
        ) + jnp.einsum("cm,cd->md", active_class, class_mlp_grad, preferred_element_type=FLOAT)
        active_back = jnp.einsum(
            "cfpd,md->cfpm", mlp_grad, return_weight[layer_index], preferred_element_type=FLOAT
        )
        class_active_back = jnp.einsum(
            "cd,md->cm", class_mlp_grad, return_weight[layer_index], preferred_element_type=FLOAT
        )
        hidden_back = jax.vjp(gelu_exact, hidden_rows)[1](active_back)[0].astype(HALF)
        class_hidden_back = jax.vjp(gelu_exact, hidden_class)[1](class_active_back)[0].astype(HALF)
        hidden_bias_grad = jnp.sum(hidden_back.astype(FLOAT), axis=(0, 1, 2)) + jnp.sum(
            class_hidden_back.astype(FLOAT), axis=0
        )
        hidden_weight_grad = jnp.einsum(
            "cfpd,cfpm->dm", mlp_normed, hidden_back, preferred_element_type=FLOAT
        ) + jnp.einsum(
            "cd,cm->dm", class_mlp_normed, class_hidden_back, preferred_element_type=FLOAT
        )
        normed_sum = backward_sum(
            arrange_rows(hidden_back, class_hidden_back, part_count), hidden_weight[layer_index]
        )
        normed_back, class_normed_back = split_rows(normed_sum, patch_back.shape)
        patch_step, gain_two, shift_two = norm_back(mlp_input, gains[2], shifts[2], normed_back)
        class_step, class_gain_two, class_shift_two = norm_back(
            mlp_class, gains[2], shifts[2], class_normed_back
        )
        patch_back = patch_back + patch_step
        class_back = class_back + class_step
        gain_two = gain_two + first_part * class_gain_two
        shift_two = shift_two + first_part * class_shift_two
        bias_two = jnp.sum(patch_back, axis=(0, 1, 2)) + first_part * jnp.sum(class_back, axis=0)
        space_grad = gather_grads(patch_back.astype(HALF))
        class_space_grad = class_back.astype(HALF)
        space_proj_grad = jnp.einsum(
            "cfpe,cfpd->ed", patch_mixed, space_grad, preferred_element_type=FLOAT
        ) + jnp.einsum("ce,cd->ed", class_mixed, class_space_grad, preferred_element_type=FLOAT)
        mixed_back = jnp.einsum(
            "cfpd,ed->cfpe", space_grad, output_weight[layer_index, 1], preferred_element_type=FLOAT
        ).astype(HALF)
        class_mixed_back = jnp.einsum(
            "cd,ed->ce",
            class_space_grad,
            output_weight[layer_index, 1],
            preferred_element_type=FLOAT,
        ).astype(HALF)
        class_spread = (class_mixed_back.astype(FLOAT) / frame_count).astype(HALF)
        query_back, key_back, value_back = attend_back(
            frame_sequences(space_qkv[..., 0, :], class_qkv[:, 0], local_heads),
            frame_sequences(space_qkv[..., 1, :], class_qkv[:, 1], local_heads),
            frame_sequences(space_qkv[..., 2, :], class_qkv[:, 2], local_heads),
            space_allowed,
            space_total,
            frame_sequences(mixed_back, class_spread, local_heads),
        )
        query_rows = sequence_rows(query_back)
        key_rows = sequence_rows(key_back)
        value_rows = sequence_rows(value_back)
        patch_qkv_back = jnp.stack(
            [query_rows[:, :, 1:], key_rows[:, :, 1:], value_rows[:, :, 1:]], axis=3
        ).astype(HALF)
        class_qkv_back = jnp.stack(
            [
                jnp.sum(query_rows[:, :, 0], axis=1),
                jnp.sum(key_rows[:, :, 0], axis=1),
                jnp.sum(value_rows[:, :, 0], axis=1),
            ],
            axis=1,
        ).astype(HALF)
        space_bias_grad = qkv_bias_grad(patch_qkv_back, class_qkv_back)
        space_weight_grad = jnp.einsum(
            "cfpd,cfpje->dje", space_normed, patch_qkv_back, preferred_element_type=FLOAT
        ) + jnp.einsum("cd,cje->dje", class_normed, class_qkv_back, preferred_element_type=FLOAT)
        flat_patch = patch_qkv_back.reshape(clip_count, frame_count, patch_count, 3 * local_width)
        flat_class = class_qkv_back.reshape(clip_count, 3 * local_width)
        normed_sum = backward_sum(
            arrange_rows(flat_patch, flat_class, part_count),
            input_weight[layer_index, 1].reshape(model_width, 3 * local_width),
        )
        normed_back, class_normed_back = split_rows(normed_sum, patch_back.shape)
        patch_step, gain_one, shift_one = norm_back(space_input, gains[1], shifts[1], normed_back)
        class_step, class_gain_one, class_shift_one = norm_back(
            class_input, gains[1], shifts[1], class_normed_back
        )
        patch_back = patch_back + patch_step
        class_back = class_back + class_step
        gain_one = gain_one + first_part * class_gain_one
        shift_one = shift_one + first_part * class_shift_one
        bias_one = jnp.sum(patch_back, axis=(0, 1, 2))
        mixer_in = patch_back.astype(HALF)
        mixer_grad = jnp.einsum("cfpe,cfpd->ed", time_proj, mixer_in, preferred_element_type=FLOAT)
        proj_back = jnp.einsum(
            "cfpd,ed->cfpe", mixer_in, time_mixer[layer_index], preferred_element_type=FLOAT
        ).astype(HALF)
        bias_zero = jnp.sum(proj_back.astype(FLOAT), axis=(0, 1, 2))
        proj_full = gather_grads(proj_back)
        time_proj_grad = jnp.einsum(
            "cfpe,cfpd->ed", time_mixed, proj_full, preferred_element_type=FLOAT
        )
        time_mixed_back = jnp.einsum(
            "cfpd,ed->cfpe", proj_full, output_weight[layer_index, 0], preferred_element_type=FLOAT
        ).astype(HALF)
        query_back, key_back, value_back = attend_back(
            time_sequences(time_qkv[..., 0, :], local_heads),
            time_sequences(time_qkv[..., 1, :], local_heads),
            time_sequences(time_qkv[..., 2, :], local_heads),
            time_allowed,
            time_total,
            time_sequences(time_mixed_back, local_heads),
        )
        time_qkv_back = jnp.stack(
            [time_rows(query_back), time_rows(key_back), time_rows(value_back)], axis=3
        ).astype(HALF)
        time_bias_grad = qkv_bias_grad(time_qkv_back, None)
        time_weight_grad = jnp.einsum(
            "cfpd,cfpje->dje", time_normed, time_qkv_back, preferred_element_type=FLOAT
        )
        flat_time = time_qkv_back.reshape(clip_count, frame_count, patch_count, 3 * local_width)
        normed_sum = backward_sum(
            arrange_rows(flat_time, None, part_count),
            input_weight[layer_index, 0].reshape(model_width, 3 * local_width),
        )
        patch_step, gain_zero, shift_zero = norm_back(
            time_input, gains[0], shifts[0], normed_sum.reshape(patch_back.shape)
        )
        patch_back = patch_back + patch_step
        wide_input_weight = jnp.stack([time_weight_grad, space_weight_grad])
        wide_input_bias = jnp.stack([time_bias_grad, space_bias_grad])
        wide_output_weight = jnp.stack([time_proj_grad, space_proj_grad])
        shared_gain = jnp.stack([gain_zero, gain_one, gain_two])
        shared_shift = jnp.stack([shift_zero, shift_one, shift_two])
        shared_bias = jnp.stack([bias_zero, bias_one, bias_two, bias_three])
        wide_parts[layer_index] = (
            lax.psum_scatter(wide_input_weight, "clip", scatter_dimension=1, tiled=True),
            lax.psum_scatter(wide_input_bias, "clip", scatter_dimension=2, tiled=True),
            lax.psum_scatter(wide_output_weight, "clip", scatter_dimension=2, tiled=True),
            lax.psum_scatter(hidden_weight_grad, "clip", scatter_dimension=0, tiled=True),
            lax.psum_scatter(hidden_bias_grad, "clip", scatter_dimension=0, tiled=True),
            lax.psum_scatter(return_grad, "clip", scatter_dimension=1, tiled=True),
        )
        shared_parts[layer_index] = (
            lax.psum_scatter(shared_gain, ("clip", "head"), scatter_dimension=1, tiled=True),
            lax.psum_scatter(shared_shift, ("clip", "head"), scatter_dimension=1, tiled=True),
            lax.psum_scatter(mixer_grad, ("clip", "head"), scatter_dimension=0, tiled=True),
            lax.psum_scatter(shared_bias, ("clip", "head"), scatter_dimension=1, tiled=True),
        )
    wide_stack = [jnp.stack([wide_parts[0][member]]) for member in range(6)]
    shared_stack = [jnp.stack([shared_parts[0][member]]) for member in range(4)]
    class_input_grad = lax.dynamic_slice_in_dim(class_back, head_index * width_part, width_part, 1)
    return (
        patch_out,
        class_out,
        patch_back,
        class_input_grad,
        shared_stack[0],
        shared_stack[1],
        wide_stack[0],
        wide_stack[1],
        wide_stack[2],
        shared_stack[2],
        shared_stack[3],
        wide_stack[3],
        wide_stack[4],
        wide_stack[5],
    )


def solution(mesh):
    in_specs = (
        P("clip", "head", None, None),
        P("clip", None),
        P("clip", None, None),
        P("clip", "head", None, None),
        P("clip", None),
        P(),
        P(),
        P(None, None, None, None, "head"),
        P(None, None, None, "head"),
        P(None, None, "head", None),
        P(),
        P(),
        P(None, None, "head"),
        P(None, "head"),
        P(None, "head", None),
    )
    out_specs = (
        P("clip", "head", None, None),
        P("clip", "head"),
        P("clip", "head", None, None),
        P("clip", "head"),
        P(None, None, ("clip", "head")),
        P(None, None, ("clip", "head")),
        P(None, None, "clip", None, "head"),
        P(None, None, None, ("head", "clip")),
        P(None, None, "head", "clip"),
        P(None, ("clip", "head"), None),
        P(None, None, ("clip", "head")),
        P(None, "clip", "head"),
        P(None, ("head", "clip")),
        P(None, "head", "clip"),
    )
    return jax.shard_map(
        on_device, mesh=mesh, in_specs=in_specs, out_specs=out_specs, check_vma=False
    )
```

profile of v0, /device:TPU:0, one launch (start us, length us, event | category | flops | bytes accessed | tf_op | source)
XLA Modules:
  0.0 998.3 jit_solution(10896478546841058790)
XLA Ops:
  22.6 20.0 %all-gather.18.cloned.1.call-done = bf16[1,8,196,768]{3,2,0,1:T(8,128)(2,1)} async-done(((bf16[1,2,196,768]{3,2,0,1:T(8,128)(2,1)}), bf16[1,8,196,768]{3,2,0,1:T(8,128)(2,1)}) %all-gather.18.cloned.1.call-update) | async-done | bytes 2408464 | tf_op jit(solution)/shard_map/all_gather | solution.py:128
  75.5 10.9 %all-to-all-done = bf16[4,392,192]{1,2,0:T(8,128)(2,1)S(1)} async-done(((bf16[4,392,192]{1,2,0:T(8,128)(2,1)}), bf16[4,392,192]{1,2,0:T(8,128)(2,1)S(1)}, u32[]{:S(2)}, u32[]{:S(2)}) %all-to-all-start) | async-done | bytes 602144 | tf_op jit(solution)/shard_map/all_to_all | solution.py:136
  96.0 21.1 %all-gather.20.cloned.1.call-done = bf16[1,8,196,768]{3,2,0,1:T(8,128)(2,1)} async-done(((bf16[1,2,196,768]{3,2,0,1:T(8,128)(2,1)}), bf16[1,8,196,768]{3,2,0,1:T(8,128)(2,1)}) %all-gather.20.cloned.1.call-update) | async-done | bytes 2408464 | tf_op jit(solution)/shard_map/all_gather | solution.py:128
  127.0 6.5 copy.137
  137.5 8.4 fusion.13
  165.9 11.6 %all-to-all-done.1 = bf16[4,393,192]{1,2,0:T(8,128)(2,1)} async-done(((bf16[4,393,192]{1,2,0:T(8,128)(2,1)}), bf16[4,393,192]{1,2,0:T(8,128)(2,1)}, u32[]{:S(2)}, u32[]{:S(2)}) %all-to-all-start.1) | async-done | bytes 603680 | tf_op jit(solution)/shard_map/all_to_all | solution.py:136
  203.9 9.5 all-gather.22.cloned.1.call-done
  221.2 12.2 %multiply_convert_fusion = (bf16[8,196,768]{2,1,0:T(8,128)(2,1)}, f32[8,196,768]{2,1,0:T(8,128)}) fusion(f32[8,196,768]{2,1,0:T(8,128)S(1)} %get-tuple-element.169, f32[768]{0:T(1024)S(1)} %copy-done.84, u8[196,768]{1,0:T(8,128)(4,1)S(1)} %get-tuple-element.71, u8[196,768]{1,0:T(8,128)(4,1)S(1)} %get-tuple-element.70), kind=kLoop, calls=%fused_computation.11 | loop fusion | flops 85499904 | bytes 12346368 | tf_op jit(solution)/shard_map/convert_element_type | solution.py:243
  239.5 10.7 %convert_reduce_fusion = (f32[768]{0:T(1024)}, bf16[8,196,768]{2,1,0:T(8,128)(2,1)}) fusion(f32[8,196,768]{2,1,0:T(8,128)} %get-tuple-element.117, bf16[1,768,768]{2,1,0:T(8,128)(2,1)} %param.29, bf16[1,8,196,768]{3,2,0,1:T(8,128)(2,1)} %all-gather.24.cloned.1.call-done, f32[8,196,768]{2,1,0:T(8,128)} %copy-done.25, f32[768]{0:T(1024)} %reduce.65), kind=kOutput, calls=%fused_computation.9 | convolution fusion | flops 1870159104 | bytes 15636480 | tf_op jit(solution)/shard_map/cfpd,md->cfpm/dot_general | solution.py:319
  271.0 33.9 %all-to-all-done.3 = bf16[4,393,768]{2,1,0:T(8,128)(2,1)} async-done(((bf16[4,393,768]{2,1,0:T(8,128)(2,1)}), bf16[4,393,768]{2,1,0:T(8,128)(2,1)}, u32[]{:S(2)}, u32[]{:S(2)}) %all-to-all-start.3) | async-done | bytes 2414624 | tf_op jit(solution)/shard_map/all_to_all | solution.py:142
  326.1 28.9 %all-to-all-done.2 = bf16[4,393,768]{2,1,0:T(8,128)(2,1)} async-done(((bf16[4,393,768]{2,1,0:T(8,128)(2,1)}), bf16[4,393,768]{2,1,0:T(8,128)(2,1)}, u32[]{:S(2)}, u32[]{:S(2)}) %all-to-all-start.2) | async-done | bytes 2414624 | tf_op jit(solution)/shard_map/all_to_all | solution.py:136
  392.4 12.8 %all-gather.26.cloned.1.call-done = bf16[1,8,196,768]{3,2,0,1:T(8,128)(2,1)} async-done(((bf16[1,2,196,768]{3,2,0,1:T(8,128)(2,1)}), bf16[1,8,196,768]{3,2,0,1:T(8,128)(2,1)}) %all-gather.26.cloned.1.call-update) | async-done | bytes 2408464 | tf_op jit(solution)/shard_map/all_gather | solution.py:132
  412.3 7.0 copy.149
  424.7 29.8 %multiply_convert_fusion.1 = bf16[8,3,197,197]{3,0,2,1:T(8,128)(2,1)S(1)} fusion(f32[8,3,197,197]{3,0,2,1:T(8,128)S(1)} %copy-done.26, f32[8,3,197,197]{3,0,2,1:T(8,128)} %copy.137, f32[8,3,197]{0,2,1:T(8,128)S(1)} %copy-done.48, pred[8,197,197]{2,0,1:T(8,128)(4,1)S(1)} %copy-done.21), kind=kOutput, calls=%fused_computation.24 | output fusion | flops 9319084 | bytes 9643544 | tf_op jit(solution)/shard_map/sub | solution.py:51
  483.7 28.7 %all_to_all.105 = bf16[4,393,576]{2,1,0:T(8,128)(2,1)S(1)} all-to-all(bf16[4,393,576]{2,1,0:T(8,128)(2,1)} %copy.154), channel_id=1, replica_groups=mesh['clip'=8,'head'=4] {'head'}, dimensions={0} | all-to-all | bytes 3621888 | tf_op jit(solution)/shard_map/all_to_all | solution.py:142
  546.7 13.6 %all-gather.40.cloned.1.call-done = bf16[8,196,768]{2,1,0:T(8,128)(2,1)} async-done(((bf16[2,196,768]{2,1,0:T(8,128)(2,1)}), bf16[8,196,768]{2,1,0:T(8,128)(2,1)}) %all-gather.40.cloned.1.call-update) | async-done | bytes 2408464 | tf_op jit(solution)/shard_map/all_gather | solution.py:132
  606.6 6.9 copy.186
  613.5 8.0 reshape.1375
  654.7 7.1 reshape.1370
  672.7 22.7 %all-reduce.7 = (f32[2,2,192]{2,1,0:T(2,128)S(1)}, f32[768]{0:T(1024)S(1)}) all-reduce(f32[2,2,192]{2,1,0:T(2,128)S(1)} %pad_maximum_fusion.7, f32[768]{0:T(1024)S(1)} %copy-done.90), channel_id=10, replica_groups=mesh['clip'=8,'head'=4] {'clip'}, use_global_device_ids=true, to_apply=%region_41.42.clone | all-reduce | flops 1536 | bytes 12288
  715.1 39.5 %all-reduce.6 = (f32[3,768]{1,0:T(4,128)S(1)}, f32[3,768]{1,0:T(4,128)S(1)}, f32[4,768]{1,0:T(4,128)S(1)}) all-reduce(f32[3,768]{1,0:T(4,128)S(1)} %pad_maximum_fusion.2, f32[3,768]{1,0:T(4,128)S(1)} %pad_maximum_fusion.3, f32[4,768]{1,0:T(4,128)S(1)} %pad_maximum_fusion.4), channel_id=7, replica_groups=mesh['clip'=8,'head'=4] {'clip','head'}, use_global_device_ids=true, to_apply=%region_33.34.clone | all-reduce | flops 7680 | bytes 61440
  764.4 51.3 %reduce-scatter.16.cloned.1.call-done = f32[96,768]{1,0:T(8,128)} async-done(((f32[768,768]{1,0:T(8,128)}), f32[96,768]{1,0:T(8,128)}) %reduce-scatter.16.cloned.1.call-update) | async-done | bytes 294928 | tf_op jit(solution)/shard_map/reduce_scatter | solution.py:452
  815.7 72.0 %reduce-scatter.18.cloned.1.call-done = f32[768,96]{0,1:T(8,128)} async-done(((f32[768,768]{0,1:T(8,128)}), f32[768,96]{0,1:T(8,128)}) %reduce-scatter.18.cloned.1.call-update) | async-done | bytes 294928 | tf_op jit(solution)/shard_map/reduce_scatter | solution.py:454
  887.7 103.8 %reduce-scatter.14.cloned.1.call-done = f32[24,768]{1,0:T(8,128)} async-done(((f32[768,768]{1,0:T(8,128)}), f32[24,768]{1,0:T(8,128)}) %reduce-scatter.14.cloned.1.call-update) | async-done | bytes 73744 | tf_op jit(solution)/shard_map/reduce_scatter | solution.py:459
  (529 shorter events, 398.6 us)
Async XLA Ops:
  7.2 82.9 %copy-start = (bf16[1,768,768]{2,1,0:T(8,128)(2,1)S(1)}, bf16[1,768,768]{2,1,0:T(8,128)(2,1)}, u32[]{:S(2)}) copy-start(bf16[1,768,768]{2,1,0:T(8,128)(2,1)} %param.25) | copy-start | bytes 3538948
  7.2 35.4 %all-gather.18.cloned.1.call-start = ((), (), s32[]{:S(2)}) async-start(), calls=%async_computation.11 | async-start | bytes 3072000 | tf_op jit(solution)/shard_map/all_gather | solution.py:128
  15.1 72.7 %all-gather.32.cloned.1.call-start = ((), (), s32[]{:S(2)}) async-start(), calls=%async_computation.21 | async-start | bytes 1474560 | tf_op jit(solution)/shard_map/all_gather | solution.py:137
  71.4 15.1 %all-to-all-start = ((bf16[4,392,192]{1,2,0:T(8,128)(2,1)}), bf16[4,392,192]{1,2,0:T(8,128)(2,1)S(1)}, u32[]{:S(2)}, u32[]{:S(2)}) async-start(bf16[4,392,192]{1,2,0:T(8,128)(2,1)} %copy.134), calls=%async_computation | async-start | bytes 1572864 | tf_op jit(solution)/shard_map/all_to_all | solution.py:136
  74.9 42.3 %all-gather.20.cloned.1.call-start = ((), (), s32[]{:S(2)}) async-start(), calls=%async_computation.12 | async-start | bytes 3072000 | tf_op jit(solution)/shard_map/all_gather | solution.py:128
  91.2 29.9 %copy-start.63 = (f32[2,196]{1,0:T(2,128)}, f32[2,196]{1,0:T(2,128)S(1)}, u32[]{:S(2)}) copy-start(f32[2,196]{1,0:T(2,128)S(1)} %fusion.201) | copy-start | bytes 4708
  92.3 73.6 %all-gather.34.cloned.1.call-start = ((), (), s32[]{:S(2)}) async-start(), calls=%async_computation.22 | async-start | bytes 1474560 | tf_op jit(solution)/shard_map/all_gather | solution.py:137
  161.6 15.9 %all-to-all-start.1 = ((bf16[4,393,192]{1,2,0:T(8,128)(2,1)}), bf16[4,393,192]{1,2,0:T(8,128)(2,1)}, u32[]{:S(2)}, u32[]{:S(2)}) async-start(bf16[4,393,192]{1,2,0:T(8,128)(2,1)} %copy.140), calls=%async_computation.1 | async-start | bytes 1572864 | tf_op jit(solution)/shard_map/all_to_all | solution.py:136
  165.8 47.6 %all-gather.22.cloned.1.call-start = ((), (), s32[]{:S(2)}) async-start(), calls=%async_computation.13 | async-start | bytes 3072000 | tf_op jit(solution)/shard_map/all_gather | solution.py:128
  188.6 50.9 %all-gather.24.cloned.1.call-start = ((), (), s32[]{:S(2)}) async-start(), calls=%async_computation.14 | async-start | bytes 3072000 | tf_op jit(solution)/shard_map/all_gather | solution.py:132
  192.6 123.0 %all-gather.38.cloned.1.call-start = ((), (), s32[]{:S(2)}) async-start(), calls=%async_computation.24 | async-start | bytes 5898240 | tf_op jit(solution)/shard_map/all_gather | solution.py:143
  193.4 170.1 %all-gather.36.cloned.1.call-start = ((), (), s32[]{:S(2)}) async-start(), calls=%async_computation.23 | async-start | bytes 5898240 | tf_op jit(solution)/shard_map/all_gather | solution.py:137
  258.4 46.5 %all-to-all-start.3 = ((bf16[4,393,768]{2,1,0:T(8,128)(2,1)}), bf16[4,393,768]{2,1,0:T(8,128)(2,1)}, u32[]{:S(2)}, u32[]{:S(2)}) async-start(bf16[4,393,768]{2,1,0:T(8,128)(2,1)} %maximum_bitcast_fusion.1), calls=%async_computation.3 | async-start | bytes 4915200 | tf_op jit(solution)/shard_map/all_to_all | solution.py:142
  304.9 50.1 %all-to-all-start.2 = ((bf16[4,393,768]{2,1,0:T(8,128)(2,1)}), bf16[4,393,768]{2,1,0:T(8,128)(2,1)}, u32[]{:S(2)}, u32[]{:S(2)}) async-start(bf16[4,393,768]{2,1,0:T(8,128)(2,1)} %maximum_bitcast_fusion), calls=%async_computation.2 | async-start | bytes 4915200 | tf_op jit(solution)/shard_map/all_to_all | solution.py:136
  309.5 95.7 %all-gather.26.cloned.1.call-start = ((), (), s32[]{:S(2)}) async-start(), calls=%async_computation.15 | async-start | bytes 3072000 | tf_op jit(solution)/shard_map/all_gather | solution.py:132
  380.4 138.6 %all-gather.28.cloned.1.call-start = ((), (), s32[]{:S(2)}) async-start(), calls=%async_computation.16 | async-start | bytes 4423680 | tf_op jit(solution)/shard_map/all_gather | solution.py:143
  383.2 177.1 %all-gather.40.cloned.1.call-start = ((), (), s32[]{:S(2)}) async-start(), calls=%async_computation.25 | async-start | bytes 3072000 | tf_op jit(solution)/shard_map/all_gather | solution.py:132
  535.6 169.2 %all-gather.30.cloned.1.call-start = ((), (), s32[]{:S(2)}) async-start(), calls=%async_computation.17 | async-start | bytes 4423680 | tf_op jit(solution)/shard_map/all_gather | solution.py:143
  536.1 223.7 %reduce-scatter.22.cloned.1.call-start = ((), (), s32[]{:S(2)}) async-start(), calls=%async_computation.27 | async-start | bytes 1327104
  580.1 181.7 %reduce-scatter.20.cloned.1.call-start = ((), (), s32[]{:S(2)}) async-start(), calls=%async_computation.26 | async-start | bytes 3981312
  621.5 194.2 %reduce-scatter.16.cloned.1.call-start = ((), (), s32[]{:S(2)}) async-start(), calls=%async_computation.19 | async-start | bytes 2654208 | tf_op jit(solution)/shard_map/reduce_scatter | solution.py:452
  628.4 259.3 %reduce-scatter.18.cloned.1.call-start = ((), (), s32[]{:S(2)}) async-start(), calls=%async_computation.20 | async-start | bytes 2654208 | tf_op jit(solution)/shard_map/reduce_scatter | solution.py:454
  661.9 34.8 %all-to-all-start.5 = ((bf16[4,392,576]{2,1,0:T(8,128)(2,1)}), bf16[4,392,576]{2,1,0:T(8,128)(2,1)}, u32[]{:S(2)}, u32[]{:S(2)}) async-start(bf16[4,392,576]{2,1,0:T(8,128)(2,1)} %reshape.1370), calls=%async_computation.5 | async-start | bytes 4014080 | tf_op jit(solution)/shard_map/all_to_all | solution.py:142
  666.5 325.1 %reduce-scatter.14.cloned.1.call-start = ((), (), s32[]{:S(2)}) async-start(), calls=%async_computation.18 | async-start | bytes 2433024 | tf_op jit(solution)/shard_map/reduce_scatter | solution.py:459
  (121 other events, 446.3 us)
Sparse Core Ops, SparseCore 0:
  15.2 27.3 all-gather.17
  44.7 17.4 all-gather.31
  92.5 24.6 all-gather.19
  119.1 17.4 all-gather.33
  188.7 24.6 all-gather.21
  214.8 24.6 all-gather.23
  241.1 48.3 all-gather.37
  291.0 54.8 all-gather.35
  380.5 24.6 all-gather.25
  407.2 30.7 all-gather.27
  535.7 24.6 all-gather.39
  561.8 30.7 all-gather.29
  596.0 64.0 reduce-scatter.21
  663.5 79.2 reduce-scatter.19
  746.8 68.8 reduce-scatter.15
  819.6 68.0 reduce-scatter.17
  893.4 98.0 reduce-scatter.13
where the time goes:
time: 1010 us; the launch traced here: 998 us
  waiting for transfers between devices  398 us (39%)
  local copies, waits for them, and re-layouts  203 us (20%)
  other arithmetic  137 us (14%)
  matrix products  124 us (12%)
  blocking collectives  90.9 us (9%)
  starting transfers between devices  22.9 us (2%)
  between operations  22.6 us (2%)
    reduce_scatter x1, waiting for transfers between devices, on_device(): lax.psum_scatter(mixer_grad, ('clip', 'head'), scatter_dimension=0, tiled...  104 us
    reduce_scatter x1, waiting for transfers between devices, on_device(): lax.psum_scatter(return_grad, 'clip', scatter_dimension=1, tiled=True)  72 us
    unnamed x2, blocking collectives  62.2 us
    unnamed x262, local copies, waits for them, and re-layouts  59.1 us
    all_to_all x3, waiting for transfers between devices, forward_sum(): lax.all_to_all(arranged, 'head', split_axis=0, concat_axis=1, tiled=True)  51.5 us
    reduce_scatter x1, waiting for transfers between devices, on_device(): lax.psum_scatter(hidden_weight_grad, 'clip', scatter_dimension=0, tiled=T...  51.3 us
    all_gather x3, waiting for transfers between devices, gather_rows(): return lax.all_gather(normed, 'head', axis=1, tiled=True)  50.6 us
    all_to_all x2, waiting for transfers between devices, backward_sum(): lax.all_to_all(arranged, 'head', split_axis=0, concat_axis=1, tiled=True)  33.9 us
  transfers between devices with their start and end apart: 22, of which 13 were waited for; matrix products, arithmetic and copies ran while one was open for 38% of the time, Pallas kernels for 0%

commit v1 on v0

v1 whole, which is shorter than its diff:
```python
import functools

import jax
import jax.numpy as jnp
from jax import lax
from jax.experimental import pallas as pl
from jax.experimental.pallas import tpu as pltpu
from jax.sharding import PartitionSpec as P

HEAD_DIM = 64
PAIR = 2 * HEAD_DIM
TILE = 16
EPSILON = 1e-06
MASKED = -1e30
FLOAT = jnp.float32
HALF = jnp.bfloat16
ROW_ROW = (((1,), (1,)), ((), ()))
COL_COL = (((0,), (0,)), ((), ()))
ROOT_HALF = 0.7071067811865476
ROOT_TWO_PI = 0.3989422804014327


def round_up(value, unit):
    return -(-value // unit) * unit


def mm(left, right):
    return jnp.dot(left, right, preferred_element_type=FLOAT)


def mm_t(left, right):
    return lax.dot_general(left, right, ROW_ROW, preferred_element_type=FLOAT)


def t_mm(left, right):
    return lax.dot_general(left, right, COL_COL, preferred_element_type=FLOAT)


def normalize(values):
    average = jnp.mean(values, axis=-1, keepdims=True)
    centred = values - average
    spread = jnp.mean(centred * centred, axis=-1, keepdims=True)
    inverse = lax.rsqrt(spread + EPSILON)
    return centred * inverse, inverse


def normalize_back(scaled, unit, inverse):
    first = jnp.mean(scaled, axis=-1, keepdims=True)
    second = jnp.mean(scaled * unit, axis=-1, keepdims=True)
    return (scaled - first - unit * second) * inverse


def rows_iota(shape):
    return lax.broadcasted_iota(jnp.int32, shape, 0)


def lanes_iota(shape):
    return lax.broadcasted_iota(jnp.int32, shape, 1)


def half_masks():
    lanes = lanes_iota((1, PAIR))
    first = (lanes < HEAD_DIM).astype(HALF)
    return first, (1 - first).astype(HALF)


def softmax_columns(scores):
    top = jnp.max(scores, axis=0, keepdims=True)
    exponent = jnp.exp(scores - top)
    total = jnp.sum(exponent, axis=0, keepdims=True)
    return exponent * (1.0 / total)


def time_norm_kernel(tokens, gains, shifts, out):
    frames, patches, _ = tokens.shape
    rows = out.shape[1]
    for frame in range(frames):
        unit, _ = normalize(tokens[frame].astype(FLOAT))
        out[frame, :patches] = (unit * gains[...] + shifts[...]).astype(HALF)
        out[frame, patches:] = jnp.zeros((rows - patches, out.shape[2]), HALF)


def group_allowed(keep_columns, group):
    shape = (keep_columns.shape[0],) * 2
    key, query = rows_iota(shape), lanes_iota(shape)
    chosen = lanes_iota(keep_columns.shape) == group
    kept = jnp.sum(jnp.where(chosen, keep_columns, 0.0), axis=1, keepdims=True)
    same = lax.rem(key, TILE) == lax.rem(query, TILE)
    return same & ((kept > 0.5) | (key == query))


def time_forward_kernel(heads, blocks, *refs):
    normed = refs[:blocks]
    weight, query_bias, value_bias, keep = refs[blocks : blocks + 4]
    outs = refs[blocks + 4 : 2 * blocks + 4]
    qkv, weights_out = refs[2 * blocks + 4 :]
    frames, rows, width = normed[0].shape
    wide = query_bias.shape[1]
    group_rows = blocks * frames * TILE
    for block in range(blocks):
        mixed = mm_t(normed[block][...].reshape(frames * rows, width), weight[...])
        part = qkv.at[block * frames : (block + 1) * frames]
        query = (mixed[:, :wide] + query_bias[...]).astype(HALF) * (HEAD_DIM**-0.5)
        part[:, :, :wide] = query.astype(HALF).reshape(frames, rows, wide)
        part[:, :, wide : 2 * wide] = (
            mixed[:, wide : 2 * wide].astype(HALF).reshape(frames, rows, wide)
        )
        part[:, :, 2 * wide :] = (
            (mixed[:, 2 * wide :] + value_bias[...]).astype(HALF).reshape(frames, rows, wide)
        )
    keep_columns = keep[...].T
    masks = half_masks()

    def one_group(group, carry):
        spot = pl.ds(pl.multiple_of(group * TILE, TILE), TILE)
        piece = qkv[:, spot, :].reshape(group_rows, 3 * wide)
        allowed = group_allowed(keep_columns, group)
        found = []
        for pair in range(wide // PAIR):
            query = piece[:, pair * PAIR : (pair + 1) * PAIR]
            key = piece[:, wide + pair * PAIR : wide + (pair + 1) * PAIR]
            value = piece[:, 2 * wide + pair * PAIR : 2 * wide + (pair + 1) * PAIR]
            total = jnp.zeros((group_rows, PAIR), FLOAT)
            for side in range(2):
                head = 2 * pair + side
                if head >= heads:
                    continue
                scores = mm_t(key * masks[side], query)
                soft = softmax_columns(jnp.where(allowed, scores, MASKED)).astype(HALF)
                weights_out[group, head] = soft
                total = total + t_mm(soft, value * masks[side])
            found.append(total.astype(HALF))
        joined = jnp.concatenate(found, axis=1)[:, : heads * HEAD_DIM]
        joined = joined.reshape(blocks, frames, TILE, heads * HEAD_DIM)
        for block in range(blocks):
            outs[block][:, spot, :] = joined[block]
        return carry

    lax.fori_loop(0, rows // TILE, one_group, 0)


def gather_rows(dest, parts, first, count):
    for place, part in enumerate(parts):
        dest[place * count : (place + 1) * count, :] = part[first : first + count, :]


def space_forward_kernel(blocks, own_width, *refs):
    tokens, class_token = refs[:2]
    mixed = refs[2 : 2 + blocks]
    bundles = refs[2 + blocks : 2 + 2 * blocks]
    mixer, biases, gains, shifts, query_bias, value_bias, keep = refs[
        2 + 2 * blocks : 9 + 2 * blocks
    ]
    (state_out, proj_out, normed_out, query_out, key_out, value_out, weights_out, spread_out,
     next_out, class_out) = refs[9 + 2 * blocks : 19 + 2 * blocks]
    joint, blocked = refs[19 + 2 * blocks :]
    frames, patches, width = tokens.shape
    rows = state_out.shape[1]
    flat = (frames * rows, width)
    total = jnp.zeros(flat, FLOAT)
    for block in range(blocks):
        total = total + mm(
            mixed[block][...].reshape(frames * rows, own_width), bundles[block][:own_width, :]
        )
    proj = (total + biases[0:1, :]).astype(HALF)
    proj_out[...] = proj.reshape(frames, rows, width)
    added = (mm(proj, mixer[...]) + biases[1:2, :]).reshape(frames, rows, width)
    for frame in range(frames):
        state_out[frame, :patches] = tokens[frame].astype(FLOAT) + added[frame, :patches]
        state_out[frame, patches : patches + 1] = class_token[...].astype(FLOAT)
        state_out[frame, patches + 1 :] = jnp.zeros((rows - patches - 1, width), FLOAT)
    unit, _ = normalize(state_out[...].reshape(flat))
    real = lax.rem(rows_iota((frames * rows, 1)), rows) <= patches
    normed = jnp.where(real, unit * gains[1:2, :] + shifts[1:2, :], 0.0).astype(HALF)
    normed_out[...] = normed.reshape(frames, rows, width)
    for kind, (dest, bias) in enumerate(
        ((query_out, query_bias), (key_out, None), (value_out, value_bias))
    ):
        gather_rows(joint, bundles, (1 + kind) * own_width, own_width)
        raw = mm_t(normed, joint[...])
        if bias is not None:
            raw = raw + bias[...]
        raw = raw.astype(HALF)
        if kind == 0:
            raw = (raw * (HEAD_DIM**-0.5)).astype(HALF)
        dest[...] = raw.reshape(frames, rows, width)
    key_index, query_index = rows_iota((rows, rows)), lanes_iota((rows, rows))
    for frame in range(frames):
        allowed = (
            (keep[:, frame : frame + 1] > 0.5) | (key_index == patches) | (key_index == query_index)
        )
        blocked[frame] = jnp.where(allowed, 0.0, MASKED)
    masks = half_masks()
    for frame in range(frames):

        def one_pair(pair, carry):
            spot = pl.ds(pl.multiple_of(pair * PAIR, PAIR), PAIR)
            query, key, value = query_out[frame, :, spot], key_out[frame, :, spot], value_out[frame, :, spot]
            total = jnp.zeros((rows, PAIR), FLOAT)
            for side in range(2):
                scores = mm_t(key * masks[side], query) + blocked[frame]
                soft = softmax_columns(scores).astype(HALF)
                weights_out[frame, 2 * pair + side] = soft
                total = total + t_mm(soft, value * masks[side])
            spread_out[frame, :, spot] = total.astype(HALF)
            return carry

        lax.fori_loop(0, width // PAIR, one_pair, 0)
    gather_rows(joint, bundles, 4 * own_width, own_width)
    added = mm(spread_out[...].reshape(flat), joint[...]).reshape(frames, rows, width)
    next_out[...] = state_out[...] + added + biases[2:3, :]
    part = added[0, patches : patches + 1]
    for frame in range(1, frames):
        part = part + added[frame, patches : patches + 1]
    class_out[...] = part * (1.0 / (frames * blocks))


def gelu_parts(values):
    size = jnp.abs(values)
    density = jnp.exp(-0.5 * values * values)
    step = 1.0 / (1.0 + (0.3275911 * ROOT_HALF) * size)
    tail = step * (
        0.5 * 0.254829592
        + step
        * (
            0.5 * -0.284496736
            + step * (0.5 * 1.421413741 + step * (0.5 * -1.453152027 + step * (0.5 * 1.061405429)))
        )
    )
    tail = tail * density
    return jnp.where(values < 0.0, tail, 1.0 - tail), density * ROOT_TWO_PI


def mlp_kernel(order, steps_per, *refs):
    blocks = len(order)
    index, state, class_token = refs[:3]
    class_parts = refs[3 : 3 + blocks]
    grads, class_grad, keep, biases, gains, shifts = refs[3 + blocks : 9 + blocks]
    first_weights = refs[9 + blocks : 9 + 2 * blocks]
    second_weights = refs[9 + 2 * blocks : 9 + 3 * blocks]
    hidden_biases = refs[9 + 3 * blocks : 9 + 4 * blocks]
    patch_out, class_out, grad_out, sums_out, hidden_sums, sent, kept = refs[
        9 + 4 * blocks : 16 + 4 * blocks
    ]
    (full, normed, grads_half, normed_t, grads_t, first, second, bias, hidden, back, active,
     hidden_back, total, normed_back) = refs[16 + 4 * blocks :]
    frames, rows, width = state.shape
    patches = grads.shape[1]
    flat = (frames * rows, width)
    cuts, cut = normed_t.shape[:2]
    block_width = first.shape[2]
    step = pl.program_id(0)
    last = pl.num_programs(0) - 1
    lead = (index[1] == 0).astype(FLOAT)
    row = rows_iota((frames * rows, 1))
    is_class = row == patches
    is_real = (lax.rem(row, rows) < patches) | is_class

    @pl.when(step == 0)
    def _():
        full[...] = state[...]
        class_state = class_token[...].astype(FLOAT) + biases[2:3, :]
        for part in class_parts:
            class_state = class_state + part[...]
        full[0, patches : patches + 1] = class_state
        unit, _ = normalize(full[...].reshape(flat))
        values = jnp.where(is_real, unit * gains[2:3, :] + shifts[2:3, :], 0.0)
        normed[...] = values.astype(HALF)
        weighted = jnp.where(is_class, values * lead, values).astype(HALF).T
        for frame in range(frames):
            grad_out[frame, :patches] = grads[frame].astype(FLOAT) * keep[:patches, frame : frame + 1]
            grad_out[frame, patches:] = jnp.zeros((rows - patches, width), FLOAT)
        grad_out[0, patches : patches + 1] = class_grad[...].astype(FLOAT)
        values = grad_out[...].reshape(flat)
        grads_half[...] = values.astype(HALF)
        turned = jnp.where(is_class, values * lead, values)
        sums_out[2:3] = jnp.sum(turned, axis=0, keepdims=True)
        turned = turned.astype(HALF).T
        for part in range(cuts):
            place = jnp.bitwise_xor(part, index[0])
            normed_t[place] = weighted[part * cut : (part + 1) * cut]
            grads_t[place] = turned[part * cut : (part + 1) * cut]
        total[...] = jnp.zeros_like(total)
        normed_back[...] = jnp.zeros_like(normed_back)
        for scratch in (first, second, hidden, back, active, hidden_back):
            scratch[...] = jnp.zeros_like(scratch)

    for place, block in enumerate(order):

        @pl.when((step >= place * steps_per) & (step < (place + 1) * steps_per))
        def _():
            slot = lax.rem(step, 3)
            first[slot] = first_weights[block][...]
            second[slot] = second_weights[block][...]
            bias[...] = hidden_biases[block][...]

    now, before, oldest = lax.rem(step, 3), lax.rem(step + 2, 3), lax.rem(step + 1, 3)
    even, odd = lax.rem(step, 2), lax.rem(step + 1, 2)
    active_old, back_old = active[even], hidden_back[even]
    total[...] += mm(active_old, second[oldest])
    normed_back[...] += mm_t(back_old, first[oldest])
    first_grad = mm(normed_t[...].reshape(width, frames * rows), back_old)
    second_grad = mm(grads_t[...].reshape(width, frames * rows), active_old)
    joined = jnp.concatenate([first_grad.astype(HALF), second_grad.astype(HALF)], axis=1)
    joined = joined.reshape(cuts, cut, 2 * block_width)
    in_sent = step < 2 + (blocks // 2) * steps_per

    @pl.when(in_sent)
    def _():
        sent[0] = joined

    @pl.when(jnp.logical_not(in_sent))
    def _():
        kept[0] = joined

    weights_row = jnp.where(is_class, lead, 1.0)
    hidden_sums[...] = jnp.sum(back_old.astype(FLOAT) * weights_row, axis=0, keepdims=True)[None]
    inner = hidden[odd]
    chance, density = gelu_parts(inner)
    active[odd] = (inner * chance).astype(HALF)
    hidden_back[odd] = (back[odd] * (chance + inner * density)).astype(HALF)
    hidden[even] = mm(normed[...], first[now]) + bias[...]
    back[even] = mm_t(grads_half[...], second[now])

    @pl.when(step == last)
    def _():
        result = (full[...].reshape(flat) + total[...] + biases[3:4, :]).reshape(frames, rows, width)
        for frame in range(frames):
            patch_out[frame] = result[frame, :patches] * keep[:patches, frame : frame + 1]
        class_out[...] = result[0, patches : patches + 1]
        unit, inverse = normalize(full[...].reshape(flat))
        incoming = normed_back[...]
        weighted = jnp.where(is_class, incoming * lead, incoming)
        sums_out[0:1] = jnp.sum(weighted * unit, axis=0, keepdims=True)
        sums_out[1:2] = jnp.sum(weighted, axis=0, keepdims=True)
        sums_out[3:] = jnp.zeros((sums_out.shape[0] - 3, width), FLOAT)
        change = normalize_back(incoming * gains[2:3, :], unit, inverse)
        change = jnp.where(is_real, change, 0.0)
        grad_out[...] += change.reshape(frames, rows, width)


def space_backward_kernel(blocks, own_width, patches, *refs):
    (index, grads, state, query_in, key_in, value_in, weights_in, mixer, gains) = refs[:9]
    bundles = refs[9 : 9 + blocks]
    (grad_out, proj_back, spread_grad, query_back, key_back, value_back, time_grad, class_back,
     sums_out) = refs[9 + blocks : 18 + blocks]
    joint, mixed_back = refs[18 + blocks :]
    frames, rows, width = state.shape
    flat = (frames * rows, width)
    lead = (index[1] == 0).astype(FLOAT)
    row = lax.rem(rows_iota((frames * rows, 1)), rows)
    is_patch = row < patches
    share = 1.0 / (frames * blocks)
    class_grad = grads[0, patches : patches + 1]
    values = grads[...].reshape(flat)
    sums_out[2:3] = (
        jnp.sum(jnp.where(is_patch, values, 0.0), axis=0, keepdims=True) + lead * class_grad
    )
    values = jnp.where(is_patch, values, jnp.where(row == patches, class_grad * share, 0.0))
    half = values.astype(HALF)
    spread_grad[...] = half.reshape(frames, rows, width)
    gather_rows(joint, bundles, 4 * own_width, own_width)
    mixed_back[...] = mm_t(half, joint[...]).astype(HALF).reshape(frames, rows, width)
    masks = half_masks()
    for frame in range(frames):

        def one_pair(pair, carry):
            spot = pl.ds(pl.multiple_of(pair * PAIR, PAIR), PAIR)
            query, key, value = query_in[frame, :, spot], key_in[frame, :, spot], value_in[frame, :, spot]
            outer = mixed_back[frame, :, spot]
            sums = [jnp.zeros((rows, PAIR), FLOAT) for _ in range(3)]
            for side in range(2):
                soft = weights_in[frame, 2 * pair + side]
                mine = outer * masks[side]
                sums[2] = sums[2] + mm(soft, mine)
                weight_back = mm_t(value, mine)
                wide = soft.astype(FLOAT)
                product = wide * weight_back
                score_back = product - wide * jnp.sum(product, axis=0, keepdims=True)
                score_back = score_back.astype(HALF)
                sums[1] = sums[1] + mm(score_back, query * masks[side])
                sums[0] = sums[0] + t_mm(score_back, key * masks[side])
            query_back[frame, :, spot] = (sums[0] * (HEAD_DIM**-0.5)).astype(HALF)
            key_back[frame, :, spot] = sums[1].astype(HALF)
            value_back[frame, :, spot] = sums[2].astype(HALF)
            return carry

        lax.fori_loop(0, width // PAIR, one_pair, 0)
    incoming = jnp.zeros(flat, FLOAT)
    for kind, source in enumerate((query_back, key_back, value_back)):
        gather_rows(joint, bundles, (1 + kind) * own_width, own_width)
        piece = source[...].reshape(flat)
        incoming = incoming + mm(piece, joint[...])
        if kind != 1:
            sums_out[5 + kind // 2 : 6 + kind // 2] = jnp.sum(
                piece.astype(FLOAT), axis=0, keepdims=True
            )
    unit, inverse = normalize(state[...].reshape(flat))
    sums_out[0:1] = jnp.sum(incoming * unit, axis=0, keepdims=True)
    sums_out[1:2] = jnp.sum(incoming, axis=0, keepdims=True)
    shaped = incoming.reshape(frames, rows, width)
    part = shaped[0, patches : patches + 1]
    for frame in range(1, frames):
        part = part + shaped[frame, patches : patches + 1]
    class_back[...] = part
    change = normalize_back(incoming * gains[1:2, :], unit, inverse)
    result = jnp.where(is_patch, grads[...].reshape(flat) + change, 0.0)
    grad_out[...] = result.reshape(frames, rows, width)
    sums_out[3:4] = jnp.sum(result, axis=0, keepdims=True)
    half = result.astype(HALF)
    time_grad[...] = half.reshape(frames, rows, width)
    back = mm_t(half, mixer[...]).astype(HALF)
    proj_back[...] = back.reshape(frames, rows, width)
    sums_out[4:5] = jnp.sum(back.astype(FLOAT), axis=0, keepdims=True)
    sums_out[7:8] = jnp.zeros((1, width), FLOAT)


def space_weights_kernel(order, own_width, *refs):
    (index, normed, query_back, key_back, value_back, spread_grad, spread, proj, time_grad) = refs[:9]
    sent, kept, mixer_grad = refs[9:]
    frames, rows, width = normed.shape
    blocks = len(order)
    cuts, cut = mixer_grad.shape[:2]
    flat = (frames * rows, width)

    def store(found, kind):
        found = found.astype(HALF)
        for part in range(cuts):
            place = jnp.bitwise_xor(part, index[0])
            piece = found[part * cut : (part + 1) * cut]
            if kind is None:
                mixer_grad[place] = piece
                continue
            for spot, block in enumerate(order):
                dest = sent if spot < blocks // 2 else kept
                dest[spot % (blocks // 2), place, :, kind * own_width : (kind + 1) * own_width] = (
                    piece[:, block * own_width : (block + 1) * own_width]
                )

    turned = normed[...].reshape(flat).T
    for kind, source in enumerate((query_back, key_back, value_back)):
        store(mm(turned, source[...].reshape(flat)), kind)
    turned = spread_grad[...].reshape(flat).T
    store(mm(turned, spread[...].reshape(flat)), 3)
    turned = proj[...].reshape(flat).T
    store(mm(turned, time_grad[...].reshape(flat)), None)


def time_backward_kernel(heads, blocks, *refs):
    proj_back = refs[:blocks]
    normed = refs[blocks : 2 * blocks]
    qkv, weights_in, output_weight, weight, gain, shift = refs[2 * blocks : 2 * blocks + 6]
    outs = refs[2 * blocks + 6 : 3 * blocks + 6]
    qkv_back, sums_out, norm_sums, mixed_back = refs[3 * blocks + 6 :]
    frames, rows, width = proj_back[0].shape
    wide = qkv.shape[2] // 3
    own = heads * HEAD_DIM
    group_rows = blocks * frames * TILE
    for block in range(blocks):
        found = mm_t(proj_back[block][...].reshape(frames * rows, width), output_weight[...])
        mixed_back[block * frames : (block + 1) * frames, :, :own] = (
            found.astype(HALF).reshape(frames, rows, own)
        )
        mixed_back[block * frames : (block + 1) * frames, :, own:] = jnp.zeros(
            (frames, rows, wide - own), HALF
        )
    masks = half_masks()

    def one_group(group, carry):
        spot = pl.ds(pl.multiple_of(group * TILE, TILE), TILE)
        piece = qkv[:, spot, :].reshape(group_rows, 3 * wide)
        outer_all = mixed_back[:, spot, :].reshape(group_rows, wide)
        for pair in range(wide // PAIR):
            query = piece[:, pair * PAIR : (pair + 1) * PAIR]
            key = piece[:, wide + pair * PAIR : wide + (pair + 1) * PAIR]
            value = piece[:, 2 * wide + pair * PAIR : 2 * wide + (pair + 1) * PAIR]
            outer = outer_all[:, pair * PAIR : (pair + 1) * PAIR]
            sums = [jnp.zeros((group_rows, PAIR), FLOAT) for _ in range(3)]
            for side in range(2):
                head = 2 * pair + side
                if head >= heads:
                    continue
                soft = weights_in[group, head]
                mine = outer * masks[side]
                sums[2] = sums[2] + mm(soft, mine)
                weight_back = mm_t(value, mine)
                large = soft.astype(FLOAT)
                product = large * weight_back
                score_back = product - large * jnp.sum(product, axis=0, keepdims=True)
                score_back = score_back.astype(HALF)
                sums[1] = sums[1] + mm(score_back, query * masks[side])
                sums[0] = sums[0] + t_mm(score_back, key * masks[side])
            for kind, scale in enumerate((HEAD_DIM**-0.5, 1.0, 1.0)):
                value_out = (sums[kind] * scale).astype(HALF)
                start = kind * wide + pair * PAIR
                qkv_back[:, spot, start : start + PAIR] = value_out.reshape(
                    blocks * frames, TILE, PAIR
                )
        return carry

    lax.fori_loop(0, rows // TILE, one_group, 0)
    sums = jnp.zeros((1, 3 * wide), FLOAT)
    first = jnp.zeros((1, width), FLOAT)
    second = jnp.zeros((1, width), FLOAT)
    for block in range(blocks):
        piece = qkv_back[block * frames : (block + 1) * frames].reshape(frames * rows, 3 * wide)
        sums = sums + jnp.sum(piece.astype(FLOAT), axis=0, keepdims=True)
        found = mm(piece, weight[...])
        outs[block][...] = found.astype(HALF).reshape(frames, rows, width)
        values = normed[block][...].reshape(frames * rows, width).astype(FLOAT)
        first = first + jnp.sum(found * values, axis=0, keepdims=True)
        second = second + jnp.sum(found, axis=0, keepdims=True)
    sums_out[...] = sums
    norm_sums[0:1] = (first - second * shift[0:1, :]) / gain[0:1, :]
    norm_sums[1:2] = second


def time_weights_kernel(heads, blocks, *refs):
    index = refs[0]
    normed = refs[1 : 1 + blocks]
    proj_back = refs[1 + blocks : 1 + 2 * blocks]
    mixed = refs[1 + 2 * blocks : 1 + 3 * blocks]
    qkv_back, out = refs[1 + 3 * blocks :]
    frames, rows, width = normed[0].shape
    cuts, cut = out.shape[:2]
    wide = qkv_back.shape[2] // 3
    own = heads * HEAD_DIM
    tokens = frames * rows
    found = jnp.zeros((width, 3 * wide), FLOAT)
    for block in range(blocks):
        found = found + t_mm(
            normed[block][...].reshape(tokens, width),
            qkv_back[block * frames : (block + 1) * frames].reshape(tokens, 3 * wide),
        )
    other = jnp.zeros((width, own), FLOAT)
    for block in range(blocks):
        other = other + t_mm(
            proj_back[block][...].reshape(tokens, width), mixed[block][...].reshape(tokens, own)
        )
    joined = jnp.concatenate(
        [found[:, kind * wide : kind * wide + own].astype(HALF) for kind in range(3)]
        + [other.astype(HALF)],
        axis=1,
    )
    for part in range(cuts):
        out[jnp.bitwise_xor(part, index[0])] = joined[part * cut : (part + 1) * cut]


def finish_kernel(grads, tokens, back, own, other, gains, class_token, class_grad, *refs):
    class_parts, (patch_out, class_out) = refs[:-2], refs[-2:]
    frames, patches, width = tokens.shape
    for frame in range(frames):
        unit, inverse = normalize(tokens[frame].astype(FLOAT))
        incoming = (
            back[frame, :patches].astype(FLOAT)
            + own[frame, :patches].astype(FLOAT)
            + other[frame, :patches].astype(FLOAT)
        )
        patch_out[frame] = grads[frame, :patches] + normalize_back(
            incoming * gains[0:1, :], unit, inverse
        )
    unit, inverse = normalize(class_token[...].astype(FLOAT))
    incoming = class_parts[0][...]
    for part in class_parts[1:]:
        incoming = incoming + part[...]
    class_out[...] = class_grad[0, patches : patches + 1] + normalize_back(
        incoming * gains[1:2, :], unit, inverse
    )


VMEM = pl.BlockSpec(memory_space=pltpu.VMEM)
SMEM = pl.BlockSpec(memory_space=pltpu.SMEM)


def shape(dims, kind=HALF):
    return jax.ShapeDtypeStruct(tuple(dims), kind)


def call(kernel, outs, args, name, flops, scratch=(), scalars=0, **more):
    moved = sum(a.size * a.dtype.itemsize for a in args) + sum(
        o.size * o.dtype.itemsize for o in outs
    )
    return pl.pallas_call(
        kernel,
        out_shape=list(outs),
        in_specs=[SMEM] * scalars + [VMEM] * (len(args) - scalars),
        out_specs=[VMEM] * len(outs),
        scratch_shapes=list(scratch),
        cost_estimate=pl.CostEstimate(
            flops=int(flops), bytes_accessed=int(moved), transcendentals=0
        ),
        compiler_params=pltpu.CompilerParams(vmem_limit_bytes=56 * 2**20),
        name=name,
        **more,
    )(*args)


def swap(values, axis, mask):
    size = lax.axis_size(axis)
    return lax.ppermute(values, axis, [(i, i ^ mask) for i in range(size)])


def spread_blocks(values):
    near = swap(values, "head", 1)
    far = swap(values, "head", 2)
    return [values, near, far, swap(far, "head", 1)]


def halve(sent, kept, axis, mask):
    return kept.astype(FLOAT) + swap(sent, axis, mask).astype(FLOAT)


def scatter_clips(values):
    clips = values.shape[0]
    mask = 1
    while values.shape[0] > 1:
        pairs = values.reshape((values.shape[0] // 2, 2) + values.shape[1:])
        sent = pairs[:, 1].astype(HALF)
        values = halve(sent, pairs[:, 0], "clip", mask)
        mask *= 2
    assert mask == clips
    return values[0]


def scatter_heads(sent, kept):
    recv = swap(sent, "head", 1)
    near = kept[0].astype(FLOAT) + recv[0].astype(FLOAT)
    far = kept[1].astype(FLOAT) + recv[1].astype(FLOAT)
    return halve(far.astype(HALF), near, "head", 2)


def on_device(
    patch_tokens,
    class_token,
    keep_mask,
    patch_grad,
    class_grad,
    norm_gain,
    norm_bias,
    input_weight,
    input_bias,
    output_weight,
    time_mixer,
    output_bias,
    hidden_weight,
    hidden_bias,
    return_weight,
):
    blocks = lax.axis_size("head")
    clips = lax.axis_size("clip")
    head_index = lax.axis_index("head")
    clip_index = lax.axis_index("clip")
    _, frames, patches, width = patch_tokens.shape
    all_frames = keep_mask.shape[1]
    own_width = input_weight.shape[-1]
    heads = own_width // HEAD_DIM
    all_heads = heads * blocks
    hidden = hidden_weight.shape[-1]
    rows = round_up(patches + 1, TILE)
    groups = rows // TILE
    group_rows = all_frames * TILE
    wide = round_up(own_width, PAIR)
    cut = width // clips
    tokens = frames * rows
    index = jnp.stack([clip_index, head_index]).astype(jnp.int32)
    gains, shifts, biases = norm_gain[0], norm_bias[0], output_bias[0]
    patch_state, patch_back = patch_tokens[0], patch_grad[0]
    mixer = time_mixer[0]
    first_weight, second_weight = hidden_weight[0], return_weight[0]

    (time_normed,) = call(
        time_norm_kernel,
        [shape((frames, rows, width))],
        [patch_state, gains[0:1], shifts[0:1]],
        "time_norm",
        1e6,
    )
    time_blocks = spread_blocks(time_normed)

    turned = jnp.transpose(input_weight[0], (0, 2, 3, 1))
    time_weight = jnp.pad(turned[0], ((0, 0), (0, wide - own_width), (0, 0))).reshape(
        3 * wide, width
    )
    bundle = jnp.concatenate(
        [output_weight[0, 0], turned[1].reshape(3 * own_width, width), output_weight[0, 1]], axis=0
    )
    small = jnp.concatenate([input_bias[0].reshape(-1), hidden_bias[0]])[None]
    smalls = [small] + [swap(small, "head", mask) for mask in range(1, blocks)]
    bundles = spread_blocks(bundle)
    first_weights = spread_blocks(first_weight)
    second_weights = spread_blocks(second_weight)

    keep = keep_mask[0].astype(FLOAT)
    keep = jnp.pad(keep, ((0, 0), (0, rows - patches))).reshape(blocks, frames, groups, TILE)
    local_keep = lax.dynamic_index_in_dim(keep, head_index, 0, False).reshape(frames, rows).T
    order = jnp.bitwise_xor(jnp.arange(blocks), head_index)
    time_keep = jnp.transpose(jnp.take(keep, order, axis=0), (2, 0, 1, 3)).reshape(
        groups, group_rows
    )
    time_keep = jnp.pad(time_keep, ((0, round_up(groups, 8) - groups), (0, 0)))
    biases_wide = jnp.pad(input_bias[0, 0], ((0, 0), (0, wide - own_width)))

    found = call(
        functools.partial(time_forward_kernel, heads, blocks),
        [shape((frames, rows, own_width))] * blocks
        + [
            shape((all_frames, rows, 3 * wide)),
            shape((groups, heads, group_rows, group_rows)),
        ],
        [*time_blocks, time_weight, biases_wide[0:1], biases_wide[1:2], time_keep],
        "time_forward",
        6e9,
    )
    time_mixed, time_qkv, time_soft = found[:blocks], found[blocks], found[blocks + 1]
    mixed_here = [time_mixed[0]] + [
        swap(time_mixed[mask], "head", mask) for mask in range(1, blocks)
    ]

    split = 2 * own_width
    query_bias = jnp.concatenate([s[:, split : split + own_width] for s in smalls], axis=1)
    value_bias = jnp.concatenate(
        [s[:, split + own_width : 2 * split] for s in smalls], axis=1
    )
    full = (frames, rows, width)
    (state, proj, space_normed, query, key, value, space_soft, spread, next_state, class_part) = call(
        functools.partial(space_forward_kernel, blocks, own_width),
        [
            shape(full, FLOAT),
            shape(full),
            shape(full),
            shape(full),
            shape(full),
            shape(full),
            shape((frames, all_heads, rows, rows)),
            shape(full),
            shape(full, FLOAT),
            shape((1, width), FLOAT),
        ],
        [
            patch_state,
            class_token,
            *mixed_here,
            *bundles,
            mixer,
            biases,
            gains,
            shifts,
            query_bias,
            value_bias,
            local_keep,
        ],
        "space_forward",
        10e9,
        scratch=[pltpu.VMEM((width, width), HALF), pltpu.VMEM((frames, rows, rows), FLOAT)],
    )
    class_parts = [class_part] + [swap(class_part, "head", mask) for mask in range(1, blocks)]

    block_width = 256
    steps_per = hidden // block_width
    send_order = (1, 3, 0, 2)
    steps = blocks * steps_per + 2
    half_steps = (blocks // 2) * steps_per

    def fixed(dims):
        return pl.BlockSpec(dims, lambda j: (0,) * len(dims))

    def along(place, dims, axis):
        def where(j):
            spot = jnp.clip(j - place * steps_per, 0, steps_per - 1)
            return tuple(spot if a == axis else 0 for a in range(2))

        return pl.BlockSpec(dims, where)

    place_of = [send_order.index(block) for block in range(blocks)]

    def sent_at(j):
        spot = jnp.clip(j - 2, 0, half_steps - 1)
        return (spot // steps_per, 0, 0, spot % steps_per)

    def kept_at(j):
        spot = jnp.clip(j - 2 - half_steps, 0, half_steps - 1)
        return (spot // steps_per, 0, 0, spot % steps_per)

    def hidden_at(j):
        spot = jnp.clip(j - 2, 0, 2 * half_steps - 1)
        return (spot // steps_per, 0, spot % steps_per)

    hidden_biases = [s[:, 2 * split :] for s in smalls]
    piece = (1, clips, cut, 2 * block_width)
    mlp_args = [
        index,
        next_state,
        class_token,
        *class_parts,
        patch_back,
        class_grad,
        local_keep,
        biases,
        gains,
        shifts,
        *first_weights,
        *second_weights,
        *hidden_biases,
    ]
    (patch_out, class_out, grads, mlp_sums, hidden_sums, mlp_sent, mlp_kept) = pl.pallas_call(
        functools.partial(mlp_kernel, send_order, steps_per),
        grid=(steps,),
        out_shape=[
            shape((frames, patches, width), FLOAT),
            shape((1, width), FLOAT),
            shape(full, FLOAT),
            shape((8, width), FLOAT),
            shape((blocks, 1, hidden), FLOAT),
            shape((blocks // 2, clips, cut, 2 * hidden)),
            shape((blocks // 2, clips, cut, 2 * hidden)),
        ],
        in_specs=[SMEM]
        + [fixed(a.shape) for a in mlp_args[1 : 9 + blocks]]
        + [along(place_of[b], (width, block_width), 1) for b in range(blocks)]
        + [along(place_of[b], (block_width, width), 0) for b in range(blocks)]
        + [along(place_of[b], (1, block_width), 1) for b in range(blocks)],
        out_specs=[
            fixed((frames, patches, width)),
            fixed((1, width)),
            fixed(full),
            fixed((8, width)),
            pl.BlockSpec((1, 1, block_width), hidden_at),
            pl.BlockSpec(piece, sent_at),
            pl.BlockSpec(piece, kept_at),
        ],
        scratch_shapes=[
            pltpu.VMEM(full, FLOAT),
            pltpu.VMEM((tokens, width), HALF),
            pltpu.VMEM((tokens, width), HALF),
            pltpu.VMEM((clips, cut, tokens), HALF),
            pltpu.VMEM((clips, cut, tokens), HALF),
            pltpu.VMEM((3, width, block_width), HALF),
            pltpu.VMEM((3, block_width, width), HALF),
            pltpu.VMEM((1, block_width), FLOAT),
            pltpu.VMEM((2, tokens, block_width), FLOAT),
            pltpu.VMEM((2, tokens, block_width), FLOAT),
            pltpu.VMEM((2, tokens, block_width), HALF),
            pltpu.VMEM((2, tokens, block_width), HALF),
            pltpu.VMEM((tokens, width), FLOAT),
            pltpu.VMEM((tokens, width), FLOAT),
        ],
        cost_estimate=pl.CostEstimate(
            flops=int(12e9), bytes_accessed=int(40e6), transcendentals=0
        ),
        compiler_params=pltpu.CompilerParams(vmem_limit_bytes=56 * 2**20),
        name="feed_forward",
    )(*mlp_args)

    (grads_next, proj_back, spread_grad, query_back, key_back, value_back, time_grad, class_back,
     space_sums) = call(
        functools.partial(space_backward_kernel, blocks, own_width, patches),
        [
            shape(full, FLOAT),
            shape(full),
            shape(full),
            shape(full),
            shape(full),
            shape(full),
            shape(full),
            shape((1, width), FLOAT),
            shape((8, width), FLOAT),
        ],
        [index, grads, state, query, key, value, space_soft, mixer, gains, *bundles],
        "space_backward",
        12e9,
        scratch=[pltpu.VMEM((width, width), HALF), pltpu.VMEM(full, HALF)],
        scalars=1,
    )
    proj_blocks = spread_blocks(proj_back)
    class_backs = [class_back] + [swap(class_back, "head", mask) for mask in range(1, blocks)]
    half_shape = (blocks // 2, clips, cut, 4 * own_width)
    space_sent, space_kept, mixer_grad = call(
        functools.partial(space_weights_kernel, send_order, own_width),
        [shape(half_shape), shape(half_shape), shape((clips, cut, width))],
        [
            index,
            space_normed,
            query_back,
            key_back,
            value_back,
            spread_grad,
            spread,
            proj,
            time_grad,
        ],
        "space_weights",
        5e9,
        scalars=1,
    )

    found = call(
        functools.partial(time_backward_kernel, heads, blocks),
        [shape(full)] * blocks
        + [
            shape((all_frames, rows, 3 * wide)),
            shape((1, 3 * wide), FLOAT),
            shape((2, width), FLOAT),
        ],
        [
            *proj_blocks,
            *time_blocks,
            time_qkv,
            time_soft,
            output_weight[0, 0],
            time_weight,
            gains[0:1],
            shifts[0:1],
        ],
        "time_backward",
        6e9,
        scratch=[pltpu.VMEM((all_frames, rows, wide), HALF)],
    )
    normed_back = found[:blocks]
    time_qkv_back, time_bias_sums, time_norm_sums = found[blocks:]
    (time_weights,) = call(
        functools.partial(time_weights_kernel, heads, blocks),
        [shape((clips, cut, 4 * own_width))],
        [index, *time_blocks, *proj_blocks, *time_mixed, time_qkv_back],
        "time_weights",
        4e9,
        scalars=1,
    )
    near = swap(normed_back[1], "head", 1)
    across = normed_back[2].astype(FLOAT) + swap(normed_back[3], "head", 1).astype(FLOAT)
    far = swap(across.astype(HALF), "head", 2)
    patch_input_grad, class_input_grad = call(
        finish_kernel,
        [shape((frames, patches, width), FLOAT), shape((1, width), FLOAT)],
        [
            grads_next,
            patch_state,
            normed_back[0],
            near,
            far,
            gains,
            class_token,
            grads,
            *class_backs,
        ],
        "finish",
        1e6,
    )

    mlp_total = scatter_clips(scatter_heads(mlp_sent, mlp_kept))
    space_total = scatter_clips(scatter_heads(space_sent, space_kept))
    time_total = scatter_clips(time_weights)
    mixer_total = scatter_clips(mixer_grad)
    for mask in (1, 2):
        mixer_total = mixer_total + swap(mixer_total, "head", mask)
    share = cut // blocks
    mixer_total = lax.dynamic_slice_in_dim(mixer_total, head_index * share, share, 0)

    hidden_sums = jnp.stack([hidden_sums[send_order.index(b)] for b in range(blocks)])
    hidden_sums = jnp.take(hidden_sums[:, 0], order, axis=0)
    space_bias = jnp.take(space_sums[5:7].reshape(2, blocks, own_width), order, axis=1).reshape(
        2, width
    )
    time_bias = jnp.stack([time_bias_sums[0, :own_width], time_bias_sums[0, 2 * wide : 2 * wide + own_width]])
    time_bias = lax.dynamic_update_slice_in_dim(
        jnp.zeros((2, width), FLOAT), time_bias, head_index * own_width, 1
    )
    sums = jnp.concatenate(
        [
            time_norm_sums[0:1],
            space_sums[0:1],
            mlp_sums[0:1],
            time_norm_sums[1:2],
            space_sums[1:2],
            mlp_sums[1:2],
            space_sums[4:5],
            space_sums[3:4],
            space_sums[2:3],
            mlp_sums[2:3],
            time_bias,
            space_bias,
            hidden_sums.reshape(-1, width),
        ],
        axis=0,
    )
    for mask in (1, 2):
        sums = sums + swap(sums, "head", mask)
    mask = 1
    while mask < clips:
        sums = sums + swap(sums, "clip", mask)
        mask *= 2
    part = width // (clips * blocks)
    both = clip_index * blocks + head_index
    shared = lax.dynamic_slice_in_dim(sums[:10], both * part, part, 1)
    other = head_index * clips + clip_index
    input_bias_grad = lax.dynamic_slice_in_dim(
        sums[10:14].reshape(2, 2, width), other * part, part, 2
    )
    hidden_part = blocks * hidden // (clips * blocks)
    hidden_bias_grad = lax.dynamic_slice_in_dim(
        sums[14:].reshape(-1), other * hidden_part, hidden_part, 0
    )

    own = own_width
    joined = jnp.stack([time_total, space_total])
    input_weight_grad = joined[:, :, : 3 * own].reshape(2, cut, 3, own)
    output_weight_grad = jnp.transpose(joined[:, :, 3 * own :], (0, 2, 1))
    mlp_total = mlp_total.reshape(cut, steps_per, 2, block_width)
    hidden_weight_grad = mlp_total[:, :, 0].reshape(cut, hidden)
    return_weight_grad = mlp_total[:, :, 1].reshape(cut, hidden).T
    quarter = width // blocks
    return (
        patch_out[None],
        lax.dynamic_slice_in_dim(class_out, head_index * quarter, quarter, 1),
        patch_input_grad[None],
        lax.dynamic_slice_in_dim(class_input_grad, head_index * quarter, quarter, 1),
        shared[None, 0:3],
        shared[None, 3:6],
        input_weight_grad[None],
        input_bias_grad[None],
        output_weight_grad[None],
        mixer_total[None],
        shared[None, 6:10],
        hidden_weight_grad[None],
        hidden_bias_grad[None],
        return_weight_grad[None],
    )


def solution(mesh):
    in_specs = (
        P("clip", "head", None, None),
        P("clip", None),
        P("clip", None, None),
        P("clip", "head", None, None),
        P("clip", None),
        P(),
        P(),
        P(None, None, None, None, "head"),
        P(None, None, None, "head"),
        P(None, None, "head", None),
        P(),
        P(),
        P(None, None, "head"),
        P(None, "head"),
        P(None, "head", None),
    )
    out_specs = (
        P("clip", "head", None, None),
        P("clip", "head"),
        P("clip", "head", None, None),
        P("clip", "head"),
        P(None, None, ("clip", "head")),
        P(None, None, ("clip", "head")),
        P(None, None, "clip", None, "head"),
        P(None, None, None, ("head", "clip")),
        P(None, None, "head", "clip"),
        P(None, ("clip", "head"), None),
        P(None, None, ("clip", "head")),
        P(None, "clip", "head"),
        P(None, ("head", "clip")),
        P(None, "head", "clip"),
    )
    return jax.shard_map(
        on_device, mesh=mesh, in_specs=in_specs, out_specs=out_specs, check_vma=False
    )
```

time: 1010 us -> 463 us (0.46)
  waiting for transfers between devices: 398 us -> 207 us
  local copies, waits for them, and re-layouts: 203 us -> 59.3 us
  Pallas kernels: 0 us -> 126 us
  matrix products: 124 us -> 0 us
  other arithmetic: 137 us -> 23.3 us
  blocking collectives: 90.9 us -> 0 us
  between operations: 22.6 us -> 1.63 us
  starting transfers between devices: 22.9 us -> 41 us
    reduce_scatter x3 -> x0, waiting for transfers between devices: 227 us -> none  [the longest x1 104 us: on_device(): lax.psum_scatter(mixer_grad, ('clip', 'head'), scatter_dimension=0, tiled...]
    ppermute x0 -> x53, waiting for transfers between devices: none -> 207 us  [swap(): return lax.ppermute(values, axis, [(i, i ^ mask) for i in range(size)])]
    pallas_call x0 -> x9, Pallas kernels: none -> 126 us  [the longest x8 88.2 us: call(): pl.pallas_call(kernel, out_shape=list(outs), in_specs=[SMEM] * scalars +...]
    dot_general x37 -> x0, matrix products: 124 us -> none  [the longest x3 14.5 us: backward_sum(): lax.dot_general(rows_here, whole_weight, (((1,), (1,)), ((), ())), prefer...]
    all_to_all x5 -> x0, waiting for transfers between devices: 85.3 us -> none  [the longest x3 51.5 us: forward_sum(): lax.all_to_all(arranged, 'head', split_axis=0, concat_axis=1, tiled=True)]
    all_gather x12 -> x0, waiting for transfers between devices: 83.2 us -> none  [the longest x3 50.6 us: gather_rows(): return lax.all_gather(normed, 'head', axis=1, tiled=True)]
    unnamed x2 -> x0, blocking collectives: 62.2 us -> none
    reduce_sum x30 -> x0, other arithmetic: 44.9 us -> none  [the longest x8 10.2 us: layer_norm(): return centred * lax.rsqrt(spread + EPSILON) * gains + shifts]
  transfers between devices with their start and end apart: 22 -> 53, of which waited for: 13 -> 17; matrix products, arithmetic and copies ran while one was open for 38% -> 15% of each run, Pallas kernels for 0% -> 15%
where the time goes in v1:
time: 463 us; the launch traced here: 459 us
  waiting for transfers between devices  207 us (45%)
  Pallas kernels  126 us (27%)
  local copies, waits for them, and re-layouts  59.3 us (13%)
  starting transfers between devices  41 us (9%)
  other arithmetic  23.3 us (5%)
    ppermute x53, waiting for transfers between devices, swap(): return lax.ppermute(values, axis, [(i, i ^ mask) for i in range(size)])  207 us
    pallas_call x8, Pallas kernels, call(): pl.pallas_call(kernel, out_shape=list(outs), in_specs=[SMEM] * scalars +...  88.2 us
    ppermute x53, starting transfers between devices, swap(): return lax.ppermute(values, axis, [(i, i ^ mask) for i in range(size)])  41 us
    pallas_call x1, Pallas kernels, on_device(): pl.pallas_call(functools.partial(mlp_kernel, send_order, steps_per), grid...  37.9 us
    unnamed x99, local copies, waits for them, and re-layouts  19.6 us
    add x9, other arithmetic, halve(): return kept.astype(FLOAT) + swap(sent, axis, mask).astype(FLOAT)  12.5 us
  transfers between devices with their start and end apart: 53, of which 17 were waited for; matrix products, arithmetic and copies ran while one was open for 15% of the time, Pallas kernels for 15%

profile of v1, /device:TPU:0, one launch (start us, length us, event | category | flops | bytes accessed | tf_op | source)
XLA Modules:
  0.0 458.7 jit_solution(5981385631674473448)
XLA Ops:
  6.4 2.9 collective-permute-start.1
  15.2 40.5 %collective-permute-done.10 = f32[1,1536]{1,0:T(1,128)S(1)} collective-permute-done((f32[1,1536]{1,0:T(1,128)S(1)}, f32[1,1536]{1,0:T(1,128)S(1)}, u32[]{:S(2)}, u32[]{:S(2)}) %collective-permute-start.10) | collective-permute-done | bytes 6176 | tf_op jit(solution)/shard_map/ppermute | solution.py:600
  63.0 12.5 %time_forward.1 = (bf16[2,208,192]{2,1,0:T(8,128)(2,1)}, bf16[2,208,192]{2,1,0:T(8,128)(2,1)}, bf16[2,208,192]{2,1,0:T(8,128)(2,1)}, bf16[2,208,192]{2,1,0:T(8,1...) custom-call(bf16[2,208,768]{2,1,0:T(8,128)(2,1)} %time_norm.1.refs_0_.refs_4_.refs_1_, ...), custom_call_target="tpu_custom_call" | custom-call | flops 6000000000 | bytes 8218624 | tf_op jit(solution)/shard_map/time_forward/pallas_call | solution.py:583
  75.6 32.0 %collective-permute-done.11 = f32[1,1536]{1,0:T(1,128)S(1)} collective-permute-done((f32[1,1536]{1,0:T(1,128)S(1)}, f32[1,1536]{1,0:T(1,128)S(1)}, u32[]{:S(2)}, u32[]{:S(2)}) %collective-permute-start.11) | collective-permute-done | bytes 6176 | tf_op jit(solution)/shard_map/ppermute | solution.py:600
  111.0 6.0 %collective-permute-done.4.refs_4_ = bf16[2,208,192]{2,1,0:T(8,128)(2,1)S(1)} collective-permute-done((bf16[2,208,192]{2,1,0:T(8,128)(2,1)}, bf16[2,208,192]{2,1,0:T(8,128)(2,1)S(1)}, u32[]{:S(2)}, u32[]{:S(2)}) %collective-permute-start.4) | collective-permute-done | bytes 159776 | tf_op jit(solution)/shard_map/ppermute | solution.py:600
  121.3 18.1 %space_forward.1 = (f32[2,208,768]{2,1,0:T(8,128)}, bf16[2,208,768]{2,1,0:T(8,128)(2,1)}, bf16[2,208,768]{2,1,0:T(8,128)(2,1)}, bf16[2,208,768]{2,1,0:T(8,128)(2...) custom-call(bf16[2,196,768]{2,1,0:T(8,128)(2,1)} %bitcast.198, ...), custom_call_target="tpu_custom_call" | custom-call | flops 10000000000 | bytes 16828544 | tf_op jit(solution)/shard_map/space_forward/pallas_call | solution.py:583
  147.0 37.9 %feed_forward.1 = (f32[2,196,768]{2,1,0:T(8,128)}, f32[1,768]{1,0:T(1,128)}, f32[2,208,768]{2,1,0:T(8,128)}, f32[8,768]{1,0:T(8,128)}, f32[4,1,768]{2,1,0:T(1,12...) custom-call(s32[2]{0:T(128)} %pad_add_fusion.refs_0_, f32[2,208,768]{2,1,0:T(8,128)} %get-tuple-element.62.refs_1_, ...), custom_call_target="tpu_custom_call" | custom-call | flops 12000000000 | bytes 40000000 | tf_op jit(solution)/shard_map/feed_forward/pallas_call | solution.py:805
  184.9 17.7 %space_backward.1 = (f32[2,208,768]{2,1,0:T(8,128)}, bf16[2,208,768]{2,1,0:T(8,128)(2,1)}, bf16[2,208,768]{2,1,0:T(8,128)(2,1)}, bf16[2,208,768]{2,1,0:T(8,128)(...) custom-call(s32[2]{0:T(128)} %pad_add_fusion.refs_0_, ...), custom_call_target="tpu_custom_call" | custom-call | flops 12000000000 | bytes 18776072 | tf_op jit(solution)/shard_map/space_backward/pallas_call | solution.py:583
  204.6 8.0 %space_weights.1 = (bf16[2,8,96,768]{3,2,1,0:T(8,128)(2,1)}, bf16[2,8,96,768]{3,2,1,0:T(8,128)(2,1)}, bf16[8,96,768]{2,1,0:T(8,128)(2,1)}) custom-call(s32[2]{0:T(128)} %pad_add_fusion.refs_0_, bf16[2,208,768]{2,1,0:T(8,128)(2,1)} %get-tuple-element.89.refs_1_, bf16[2,208,768]{2,1,0:T(8,128)(2,1)} %get-tuple-element.90.refs_2_, ...), custom_call_target="tpu_custom_call" | custom-call | flops 5000000000 | bytes 11010056 | tf_op jit(solution)/shard_map/space_weights/pallas_call | solution.py:583
  233.5 6.9 %collective-permute-done.44 = bf16[2,96,768]{2,1,0:T(8,128)(2,1)S(1)} collective-permute-done((bf16[2,96,768]{2,1,0:T(8,128)(2,1)S(1)}, bf16[2,96,768]{2,1,0:T(8,128)(2,1)S(1)}, u32[]{:S(2)}, u32[]{:S(2)}) %collective-permute-start.44) | collective-permute-done | bytes 294944 | tf_op jit(solution)/shard_map/ppermute | solution.py:600
  241.4 16.9 %time_backward.1 = (bf16[2,208,768]{2,1,0:T(8,128)(2,1)}, bf16[2,208,768]{2,1,0:T(8,128)(2,1)}, bf16[2,208,768]{2,1,0:T(8,128)(2,1)}, bf16[2,208,768]{2,1,0:T(8,...) custom-call(bf16[2,208,768]{2,1,0:T(8,128)(2,1)} %get-tuple-element.73.refs_0_.refs_5_, ...), custom_call_target="tpu_custom_call" | custom-call | flops 6000000000 | bytes 15547392 | tf_op jit(solution)/shard_map/time_backward/pallas_call | solution.py:583
  265.3 2.9 copy.88
  274.4 8.2 %time_weights.1 = bf16[8,96,768]{2,1,0:T(8,128)(2,1)} custom-call(s32[2]{0:T(128)} %pad_add_fusion.refs_0_, bf16[2,208,768]{2,1,0:T(8,128)(2,1)} %time_norm.1.refs_0_.refs_4_.refs_1_, bf16[2,208,768]{2,1,0:T(8,128)(2,1)} %collective-permute-done.refs_1_.refs_5_.refs_2_, bf16[2,208,768]{2,1,0:T(8,128)(2,1)} %collective-permute-done.1.refs_2_.refs_6_.refs_3_, ...), custom_call_target="tpu_custom_call" | custom-call | flops 4000000000 | bytes 9486344 | tf_op jit(solution)/shard_map/time_weights/pallas_call | solution.py:583
  288.7 3.9 fusion
  305.9 4.6 %collective-permute-done.36 = bf16[2,96,768]{2,1,0:T(8,128)(2,1)} collective-permute-done((bf16[2,96,768]{2,1,0:T(8,128)(2,1)S(1)}, bf16[2,96,768]{2,1,0:T(8,128)(2,1)}, u32[]{:S(2)}, u32[]{:S(2)}) %collective-permute-start.36) | collective-permute-done | bytes 294944 | tf_op jit(solution)/shard_map/ppermute | solution.py:600
  311.5 60.4 %collective-permute-done.39 = bf16[8,96,768]{2,1,0:T(8,128)(2,1)} collective-permute-done((bf16[8,96,768]{2,1,0:T(8,128)(2,1)S(1)}, bf16[8,96,768]{2,1,0:T(8,128)(2,1)}, u32[]{:S(2)}, u32[]{:S(2)}) %collective-permute-start.39) | collective-permute-done | bytes 1179680 | tf_op jit(solution)/shard_map/ppermute | solution.py:600
  376.9 4.0 bitcast_add_fusion
  388.5 3.4 collective-permute-done.37
  392.2 2.9 collective-permute-done.29.refs_3_
  396.9 4.5 finish.1
  401.3 2.9 copy.89
  405.5 16.5 %collective-permute-done.50 = bf16[4,96,1536]{2,1,0:T(8,128)(2,1)} collective-permute-done((bf16[4,96,1536]{2,1,0:T(8,128)(2,1)}, bf16[4,96,1536]{2,1,0:T(8,128)(2,1)}, u32[]{:S(2)}, u32[]{:S(2)}) %collective-permute-start.50) | collective-permute-done | bytes 1179680 | tf_op jit(solution)/shard_map/ppermute | solution.py:600
  427.5 12.8 %collective-permute-done.51 = bf16[2,96,1536]{2,1,0:T(8,128)(2,1)S(1)} collective-permute-done((bf16[2,96,1536]{2,1,0:T(8,128)(2,1)S(1)}, bf16[2,96,1536]{2,1,0:T(8,128)(2,1)S(1)}, u32[]{:S(2)}, u32[]{:S(2)}) %collective-permute-start.51) | collective-permute-done | bytes 589856 | tf_op jit(solution)/shard_map/ppermute | solution.py:600
  443.1 10.6 %collective-permute-done.52 = bf16[1,96,1536]{2,1,0:T(8,128)(2,1)} collective-permute-done((bf16[1,96,1536]{2,1,0:T(8,128)(2,1)S(1)}, bf16[1,96,1536]{2,1,0:T(8,128)(2,1)}, u32[]{:S(2)}, u32[]{:S(2)}) %collective-permute-start.52) | collective-permute-done | bytes 294944 | tf_op jit(solution)/shard_map/ppermute | solution.py:600
  (299 shorter events, 119.8 us)
Async XLA Ops:
  6.4 51.0 %collective-permute-start.1 = (bf16[2,208,768]{2,1,0:T(8,128)(2,1)}, bf16[2,208,768]{2,1,0:T(8,128)(2,1)}, u32[]{:S(2)}, u32[]{:S(2)}) collective-permute-start(bf16[2,208,768]{2,1,0:T(8,128)(2,1)} %time_norm.1.refs_0_.refs_4_.refs_1_), channel_id=1, source_target_pairs={{0,2},{1,3},{2,0},{3,1},{4,6},{5,7},{6,4},{7,5},{8,10},{9,11},{10,... | collective-permute-start | bytes 1916936 | tf_op jit(solution)/shard_map/ppermute | solution.py:600
  9.3 48.4 %collective-permute-start = (bf16[2,208,768]{2,1,0:T(8,128)(2,1)}, bf16[2,208,768]{2,1,0:T(8,128)(2,1)}, u32[]{:S(2)}, u32[]{:S(2)}) collective-permute-start(bf16[2,208,768]{2,1,0:T(8,128)(2,1)} %time_norm.1.refs_0_.refs_4_.refs_1_), channel_id=1, source_target_pairs={{0,1},{1,0},{2,3},{3,2},{4,5},{5,4},{6,7},{7,6},{8,9},{9,8},{10,11... | collective-permute-start | bytes 1916936 | tf_op jit(solution)/shard_map/ppermute | solution.py:600
  11.2 46.6 %collective-permute-start.7 = (bf16[960,768]{1,0:T(8,128)(2,1)S(1)}, bf16[960,768]{1,0:T(8,128)(2,1)}, u32[]{:S(2)}, u32[]{:S(2)}) collective-permute-start(bf16[960,768]{1,0:T(8,128)(2,1)S(1)} %pad_maximum_fusion.refs_6_.refs_9_), channel_id=1, source_target_pairs={{0,2},{1,3},{2,0},{3,1},{4,6},{5,7},{6,4},{7,5},{8,10},{9,11},{10,... | collective-permute-start | bytes 4423688 | tf_op jit(solution)/shard_map/ppermute | solution.py:600
  11.9 43.8 %collective-permute-start.10 = (f32[1,1536]{1,0:T(1,128)S(1)}, f32[1,1536]{1,0:T(1,128)S(1)}, u32[]{:S(2)}, u32[]{:S(2)}) collective-permute-start(f32[1,1536]{1,0:T(1,128)S(1)} %broadcast_in_dim.72), channel_id=1, source_target_pairs={{0,2},{1,3},{2,0},{3,1},{4,6},{5,7},{6,4},{7,5},{8,10},{9,11},{10,... | collective-permute-start | bytes 18440 | tf_op jit(solution)/shard_map/ppermute | solution.py:600
  15.2 105.3 %collective-permute-start.6 = (bf16[960,768]{1,0:T(8,128)(2,1)S(1)}, bf16[960,768]{1,0:T(8,128)(2,1)}, u32[]{:S(2)}, u32[]{:S(2)}) collective-permute-start(bf16[960,768]{1,0:T(8,128)(2,1)S(1)} %pad_maximum_fusion.refs_6_.refs_9_), channel_id=1, source_target_pairs={{0,1},{1,0},{2,3},{3,2},{4,5},{5,4},{6,7},{7,6},{8,9},{9,8},{10,11... | collective-permute-start | bytes 4423688 | tf_op jit(solution)/shard_map/ppermute | solution.py:600
  55.7 53.0 %collective-permute-start.16 = (bf16[768,768]{1,0:T(8,128)(2,1)}, bf16[768,768]{1,0:T(8,128)(2,1)}, u32[]{:S(2)}, u32[]{:S(2)}) collective-permute-start(bf16[768,768]{1,0:T(8,128)(2,1)} %bitcast.226), channel_id=1, source_target_pairs={{0,2},{1,3},{2,0},{3,1},{4,6},{5,7},{6,4},{7,5},{8,10},{9,11},{10,... | collective-permute-start | bytes 3538952 | tf_op jit(solution)/shard_map/ppermute | solution.py:600
  57.5 52.7 %collective-permute-start.19 = (bf16[768,768]{1,0:T(8,128)(2,1)}, bf16[768,768]{1,0:T(8,128)(2,1)}, u32[]{:S(2)}, u32[]{:S(2)}) collective-permute-start(bf16[768,768]{1,0:T(8,128)(2,1)} %bitcast.229), channel_id=1, source_target_pairs={{0,2},{1,3},{2,0},{3,1},{4,6},{5,7},{6,4},{7,5},{8,10},{9,11},{10,... | collective-permute-start | bytes 3538952 | tf_op jit(solution)/shard_map/ppermute | solution.py:600
  57.8 63.5 %collective-permute-start.8 = (bf16[960,768]{1,0:T(8,128)(2,1)}, bf16[960,768]{1,0:T(8,128)(2,1)}, u32[]{:S(2)}, u32[]{:S(2)}) collective-permute-start(bf16[960,768]{1,0:T(8,128)(2,1)} %collective-permute-done.7.refs_8_.refs_11_), channel_id=1, source_target_pairs={{0,1},{1,0},{2,3},{3,2},{4,5},{5,4},{6,7},{7,6},{8,9},{9,8},{10,11... | collective-permute-start | bytes 4423688 | tf_op jit(solution)/shard_map/ppermute | solution.py:600
  61.6 45.9 %collective-permute-start.11 = (f32[1,1536]{1,0:T(1,128)S(1)}, f32[1,1536]{1,0:T(1,128)S(1)}, u32[]{:S(2)}, u32[]{:S(2)}) collective-permute-start(f32[1,1536]{1,0:T(1,128)S(1)} %broadcast_in_dim.72), channel_id=1, source_target_pairs={{0,3},{1,2},{2,1},{3,0},{4,7},{5,6},{6,5},{7,4},{8,11},{9,10},{10,... | collective-permute-start | bytes 18440 | tf_op jit(solution)/shard_map/ppermute | solution.py:600
  110.2 29.7 %collective-permute-start.15 = (bf16[768,768]{1,0:T(8,128)(2,1)S(1)}, bf16[768,768]{1,0:T(8,128)(2,1)S(1)}, u32[]{:S(2)}, u32[]{:S(2)}) collective-permute-start(bf16[768,768]{1,0:T(8,128)(2,1)S(1)} %bitcast.228), channel_id=1, source_target_pairs={{0,1},{1,0},{2,3},{3,2},{4,5},{5,4},{6,7},{7,6},{8,9},{9,8},{10,11... | collective-permute-start | bytes 3538952 | tf_op jit(solution)/shard_map/ppermute | solution.py:600
  117.0 24.3 %collective-permute-start.18 = (bf16[768,768]{1,0:T(8,128)(2,1)S(1)}, bf16[768,768]{1,0:T(8,128)(2,1)}, u32[]{:S(2)}, u32[]{:S(2)}) collective-permute-start(bf16[768,768]{1,0:T(8,128)(2,1)S(1)} %bitcast.231), channel_id=1, source_target_pairs={{0,1},{1,0},{2,3},{3,2},{4,5},{5,4},{6,7},{7,6},{8,9},{9,8},{10,11... | collective-permute-start | bytes 3538952 | tf_op jit(solution)/shard_map/ppermute | solution.py:600
  119.7 26.3 %collective-permute-start.17 = (bf16[768,768]{1,0:T(8,128)(2,1)}, bf16[768,768]{1,0:T(8,128)(2,1)}, u32[]{:S(2)}, u32[]{:S(2)}) collective-permute-start(bf16[768,768]{1,0:T(8,128)(2,1)} %collective-permute-done.16.refs_15_), channel_id=1, source_target_pairs={{0,1},{1,0},{2,3},{3,2},{4,5},{5,4},{6,7},{7,6},{8,9},{9,8},{10,11... | collective-permute-start | bytes 3538952 | tf_op jit(solution)/shard_map/ppermute | solution.py:600
  120.5 25.5 %collective-permute-start.20 = (bf16[768,768]{1,0:T(8,128)(2,1)}, bf16[768,768]{1,0:T(8,128)(2,1)S(1)}, u32[]{:S(2)}, u32[]{:S(2)}) collective-permute-start(bf16[768,768]{1,0:T(8,128)(2,1)} %collective-permute-done.19.refs_19_), channel_id=1, source_target_pairs={{0,1},{1,0},{2,3},{3,2},{4,5},{5,4},{6,7},{7,6},{8,9},{9,8},{10,11... | collective-permute-start | bytes 3538952 | tf_op jit(solution)/shard_map/ppermute | solution.py:600
  202.7 30.8 %collective-permute-start.22 = (bf16[2,208,768]{2,1,0:T(8,128)(2,1)}, bf16[2,208,768]{2,1,0:T(8,128)(2,1)}, u32[]{:S(2)}, u32[]{:S(2)}) collective-permute-start(bf16[2,208,768]{2,1,0:T(8,128)(2,1)} %get-tuple-element.73.refs_0_.refs_5_), channel_id=1, source_target_pairs={{0,2},{1,3},{2,0},{3,1},{4,6},{5,7},{6,4},{7,5},{8,10},{9,11},{10,... | collective-permute-start | bytes 1916936 | tf_op jit(solution)/shard_map/ppermute | solution.py:600
  204.1 36.4 %collective-permute-start.21 = (bf16[2,208,768]{2,1,0:T(8,128)(2,1)}, bf16[2,208,768]{2,1,0:T(8,128)(2,1)}, u32[]{:S(2)}, u32[]{:S(2)}) collective-permute-start(bf16[2,208,768]{2,1,0:T(8,128)(2,1)} %get-tuple-element.73.refs_0_.refs_5_), channel_id=1, source_target_pairs={{0,1},{1,0},{2,3},{3,2},{4,5},{5,4},{6,7},{7,6},{8,9},{9,8},{10,11... | collective-permute-start | bytes 1916936 | tf_op jit(solution)/shard_map/ppermute | solution.py:600
  204.5 84.1 %collective-permute-start.48 = (bf16[2,8,96,1536]{3,2,1,0:T(8,128)(2,1)}, bf16[2,8,96,1536]{3,2,1,0:T(8,128)(2,1)}, u32[]{:S(2)}, u32[]{:S(2)}) collective-permute-start(bf16[2,8,96,1536]{3,2,1,0:T(8,128)(2,1)} %get-tuple-element.101), channel_id=1, source_target_pairs={{0,1},{1,0},{2,3},{3,2},{4,5},{5,4},{6,7},{7,6},{8,9},{9,8},{10,11... | collective-permute-start | bytes 14155784 | tf_op jit(solution)/shard_map/ppermute | solution.py:600
  216.1 79.4 %collective-permute-start.38 = (bf16[2,8,96,768]{3,2,1,0:T(8,128)(2,1)}, bf16[2,8,96,768]{3,2,1,0:T(8,128)(2,1)S(1)}, u32[]{:S(2)}, u32[]{:S(2)}) collective-permute-start(bf16[2,8,96,768]{3,2,1,0:T(8,128)(2,1)} %get-tuple-element.98), channel_id=1, source_target_pairs={{0,1},{1,0},{2,3},{3,2},{4,5},{5,4},{6,7},{7,6},{8,9},{9,8},{10,11... | collective-permute-start | bytes 7077896 | tf_op jit(solution)/shard_map/ppermute | solution.py:600
  263.3 118.8 %collective-permute-start.27 = (f32[1,768]{1,0:T(1,128)}, f32[1,768]{1,0:T(1,128)}, u32[]{:S(2)}, u32[]{:S(2)}) collective-permute-start(f32[1,768]{1,0:T(1,128)} %get-tuple-element.80.refs_0_), channel_id=1, source_target_pairs={{0,1},{1,0},{2,3},{3,2},{4,5},{5,4},{6,7},{7,6},{8,9},{9,8},{10,11... | collective-permute-start | bytes 9224 | tf_op jit(solution)/shard_map/ppermute | solution.py:600
  292.6 83.8 %collective-permute-start.49 = (bf16[8,96,1536]{2,1,0:T(8,128)(2,1)}, bf16[8,96,1536]{2,1,0:T(8,128)(2,1)}, u32[]{:S(2)}, u32[]{:S(2)}) collective-permute-start(bf16[8,96,1536]{2,1,0:T(8,128)(2,1)} %fusion), channel_id=1, source_target_pairs={{0,2},{1,3},{2,0},{3,1},{4,6},{5,7},{6,4},{7,5},{8,10},{9,11},{10,... | collective-permute-start | bytes 7077896 | tf_op jit(solution)/shard_map/ppermute | solution.py:600
  296.9 75.0 %collective-permute-start.39 = (bf16[8,96,768]{2,1,0:T(8,128)(2,1)S(1)}, bf16[8,96,768]{2,1,0:T(8,128)(2,1)}, u32[]{:S(2)}, u32[]{:S(2)}) collective-permute-start(bf16[8,96,768]{2,1,0:T(8,128)(2,1)S(1)} %fusion.2), channel_id=1, source_target_pairs={{0,2},{1,3},{2,0},{3,1},{4,6},{5,7},{6,4},{7,5},{8,10},{9,11},{10,... | collective-permute-start | bytes 3538952 | tf_op jit(solution)/shard_map/ppermute | solution.py:600
  304.1 79.6 %collective-permute-start.28 = (f32[1,768]{1,0:T(1,128)}, f32[1,768]{1,0:T(1,128)S(1)}, u32[]{:S(2)}, u32[]{:S(2)}) collective-permute-start(f32[1,768]{1,0:T(1,128)} %get-tuple-element.80.refs_0_), channel_id=1, source_target_pairs={{0,2},{1,3},{2,0},{3,1},{4,6},{5,7},{6,4},{7,5},{8,10},{9,11},{10,... | collective-permute-start | bytes 9224 | tf_op jit(solution)/shard_map/ppermute | solution.py:600
  310.5 84.6 %collective-permute-start.24 = (bf16[2,208,768]{2,1,0:T(8,128)(2,1)S(1)}, bf16[2,208,768]{2,1,0:T(8,128)(2,1)S(1)}, u32[]{:S(2)}, u32[]{:S(2)}) collective-permute-start(bf16[2,208,768]{2,1,0:T(8,128)(2,1)S(1)} %copy-done.34), channel_id=1, source_target_pairs={{0,1},{1,0},{2,3},{3,2},{4,5},{5,4},{6,7},{7,6},{8,9},{9,8},{10,11... | collective-permute-start | bytes 1916936 | tf_op jit(solution)/shard_map/ppermute | solution.py:600
  382.1 22.2 %collective-permute-start.40 = (bf16[4,96,768]{2,1,0:T(8,128)(2,1)}, bf16[4,96,768]{2,1,0:T(8,128)(2,1)}, u32[]{:S(2)}, u32[]{:S(2)}) collective-permute-start(bf16[4,96,768]{2,1,0:T(8,128)(2,1)} %fusion.8), channel_id=1, source_target_pairs={{0,4},{4,0},{8,12},{12,8},{16,20},{20,16},{24,28},{28,24},{1,5},{5... | collective-permute-start | bytes 1769480 | tf_op jit(solution)/shard_map/ppermute | solution.py:600
  383.6 38.4 %collective-permute-start.50 = (bf16[4,96,1536]{2,1,0:T(8,128)(2,1)}, bf16[4,96,1536]{2,1,0:T(8,128)(2,1)}, u32[]{:S(2)}, u32[]{:S(2)}) collective-permute-start(bf16[4,96,1536]{2,1,0:T(8,128)(2,1)} %fusion.3), channel_id=1, source_target_pairs={{0,4},{4,0},{8,12},{12,8},{16,20},{20,16},{24,28},{28,24},{1,5},{5... | collective-permute-start | bytes 3538952 | tf_op jit(solution)/shard_map/ppermute | solution.py:600
  (73 other events, 1117.2 us)
